TPU v7x, 32 devices: a whole 2x2x4 slice. The times are simulated.
32 devices in a mesh: dp: 8 (over z, x), mp: 4 (over y, core).
Axes of the slice: x: 2, y: 2, z: 4, core: 2. Of those that a mesh axis runs over, the one named last changes fastest.
Arguments:
- token_owner: int32 [8192, 1], P('dp'), may hold values from 0 to 31; in each aligned block of 256 rows (0 to 255, 256 to 511, ...) at most 16 rows name the same one
- token_row: int32 [8192], P('dp'), may hold values from 0 to 2047
- long_len: int32 [8, 4], P('dp'), may hold values from 1 to 128, 384 in all within a row
- short_len: int32 [8, 16], P('dp'), may hold values from 1 to 32, 384 in all within a row
- pairing: int32 [160], replicated, may hold values from 0 to 159, each once
- embed_table: float32 [65536, 768], P(('dp', 'mp')), may hold values from -6 to 6
- first_moment: float32 [65536, 768], P(('dp', 'mp')), may hold values from -4 to 4
- second_moment: float32 [65536, 768], P(('dp', 'mp')), may hold values from 0.05 to 2
- heads_weight: bfloat16 [768, 3, 768], P(None, None, 'mp'), may hold values from -0.21875 to 0.21875
- mix_weight: bfloat16 [768, 768], P('mp'), may hold values from -0.625 to 0.625
- up_weight: bfloat16 [768, 3072], P(None, 'mp'), may hold values from -0.21875 to 0.21875
- down_weight: bfloat16 [3072, 768], P('mp'), may hold values from -0.109375 to 0.109375
- first_gain: float32 [768], replicated, may hold values from 0.1 to 1.9
- first_shift: float32 [768], replicated, may hold values from -4 to 4
- second_gain: float32 [768], replicated, may hold values from 0.1 to 1.9
- second_shift: float32 [768], replicated, may hold values from -4 to 4
- upper_grad: bfloat16 [8192, 768], P(('dp', 'mp')), may hold values from -6 to 6
Outputs:
- loss: float32 [], replicated
- block_out: bfloat16 [8192, 768], P(('dp', 'mp'))
- heads_grad: float32 [768, 3, 768], P(None, None, 'mp')
- mix_grad: float32 [768, 768], P('mp')
- up_grad: float32 [768, 3072], P(None, 'mp')
- down_grad: float32 [3072, 768], P('mp')
- first_gain_grad: float32 [768], replicated
- first_shift_grad: float32 [768], replicated
- second_gain_grad: float32 [768], replicated
- second_shift_grad: float32 [768], replicated
- table_step: float32 [65536, 768], P(('dp', 'mp'))
- first_new: float32 [65536, 768], P(('dp', 'mp'))
- second_new: float32 [65536, 768], P(('dp', 'mp'))
Inputs may be any that keep to these rules, and one draw needn't show every extreme that they name: `token_owner`: in each aligned block of 256 tokens no owner is named by more than 16 tokens, and in some blocks one owner is named by exactly 16; every owner is named by some token.
All inputs are finite; a program needn't handle non-finite values.
Results may differ from a plain program's by a relative error of at most 0.012.
The roundings to bfloat16 on the way count: a program that leaves them out, or rounds other values in their place, can miss the bound.
Values may be sent and summed in bfloat16 or wider, within the bound.
A program may use at most 128 MiB of HBM per device.

v0:
```python
import jax
import jax.numpy as jnp
import numpy as np
from jax import lax
from jax.sharding import PartitionSpec as P

HEAD = 64
LONG_LEN = 128
SHORT_LEN = 32


highest = lax.Precision.HIGHEST
first_fix = 1.0 - 0.9**10
second_fix = 1.0 - 0.95**10


def layer_norm(hidden, gain, shift):
    mean_value = jnp.mean(hidden, axis=-1, keepdims=True)
    centered = hidden - mean_value
    variance = jnp.mean(centered * centered, axis=-1, keepdims=True)
    return centered * lax.rsqrt(variance + 1e-12) * gain + shift


def exact_gelu(values):
    return jax.nn.gelu(values, approximate=False)


def ranking_loss(sentences, pairing):
    unit = sentences * lax.rsqrt(jnp.sum(sentences * sentences, axis=1, keepdims=True) + 1e-06)
    source = unit[pairing[0::2]]
    target = unit[pairing[1::2]]
    cosine = jnp.dot(source, target.T, precision=highest)
    count = cosine.shape[0]
    logits = 40.0 * (cosine - 0.3 * jnp.eye(count, dtype=jnp.float32))
    matched = jnp.diagonal(logits)
    forward_term = jnp.mean(jax.nn.logsumexp(logits, axis=1) - matched)
    backward_term = jnp.mean(jax.nn.logsumexp(logits, axis=0) - matched)
    return forward_term + backward_term


def rows_product(left, right):
    return lax.dot_general(
        left, right, (((0,), (0,)), ((), ())), preferred_element_type=jnp.float32
    )


def slot_ranks(owners, devices):
    onehot = (owners[:, None] == jnp.arange(devices, dtype=jnp.int32)[None, :]).astype(jnp.int32)
    running = jnp.cumsum(onehot, axis=0) - 1
    return jnp.sum(onehot * running, axis=1)


def row_layout(positions, long_lengths, short_lengths, half):
    long_count = long_lengths.shape[0]
    short_count = short_lengths.shape[0]
    is_long = positions < half
    short_pos = jnp.maximum(positions - half, 0)
    long_sent = jnp.minimum(positions // LONG_LEN, long_count - 1)
    short_sent = short_pos // SHORT_LEN
    offset = jnp.where(is_long, positions % LONG_LEN, short_pos % SHORT_LEN)
    long_hit = long_sent[:, None] == jnp.arange(long_count, dtype=jnp.int32)[None, :]
    short_hit = short_sent[:, None] == jnp.arange(short_count, dtype=jnp.int32)[None, :]
    long_size = jnp.sum(jnp.where(long_hit, long_lengths[None, :], 0), axis=1)
    short_size = jnp.sum(jnp.where(short_hit, short_lengths[None, :], 0), axis=1)
    sent_size = jnp.where(is_long, long_size, short_size)
    segment = jnp.where(is_long, long_sent, long_count + short_sent)
    return (segment, offset < sent_size)


def attend(query, key_part, value, allowed):
    scores = (
        jnp.einsum("bqhe,bkhe->bhqk", query, key_part, preferred_element_type=jnp.float32) * 0.125
    )
    scores = jnp.where(allowed[:, None], scores, -jnp.inf)
    top = jnp.max(scores, axis=-1, keepdims=True)
    weights = jnp.exp(scores - top)
    total = jnp.sum(weights, axis=-1, keepdims=True)
    probs = (weights / total).astype(jnp.bfloat16)
    output = jnp.einsum("bhqk,bkhe->bqhe", probs, value, preferred_element_type=jnp.float32)
    return (output, top + jnp.log(total))


def attend_back(query, key_part, value, allowed, log_total, grad_out):
    scores = (
        jnp.einsum("bqhe,bkhe->bhqk", query, key_part, preferred_element_type=jnp.float32) * 0.125
    )
    scores = jnp.where(allowed[:, None], scores, -jnp.inf)
    probs = jnp.exp(scores - log_total)
    probs_low = probs.astype(jnp.bfloat16)
    grad_value = jnp.einsum(
        "bhqk,bqhe->bkhe", probs_low, grad_out, preferred_element_type=jnp.float32
    )
    grad_probs = jnp.einsum("bqhe,bkhe->bhqk", grad_out, value, preferred_element_type=jnp.float32)
    inner = jnp.sum(probs * grad_probs, axis=-1, keepdims=True)
    grad_scores = (probs * (grad_probs - inner)).astype(jnp.bfloat16)
    grad_query = (
        jnp.einsum("bhqk,bkhe->bqhe", grad_scores, key_part, preferred_element_type=jnp.float32)
        * 0.125
    )
    grad_key = (
        jnp.einsum("bhqk,bqhe->bkhe", grad_scores, query, preferred_element_type=jnp.float32)
        * 0.125
    )
    return (grad_query, grad_key, grad_value)


def body(
    token_owner,
    token_row,
    long_len,
    short_len,
    pairing,
    embed_table,
    first_moment,
    second_moment,
    heads_weight,
    mix_weight,
    up_weight,
    down_weight,
    first_gain,
    first_shift,
    second_gain,
    second_shift,
    upper_grad,
):
    tok_dev = upper_grad.shape[0]
    width = upper_grad.shape[1]
    n_model = lax.axis_size("mp")
    n_data = lax.axis_size("dp")
    devices = n_model * n_data
    group = tok_dev * n_model
    half = group // 2
    table_rows = embed_table.shape[0]
    model_pos = lax.axis_index("mp")
    place = lax.axis_index("dp") * n_model + model_pos
    own_start = model_pos * tok_dev
    capacity = max(2, 2 * tok_dev // devices)
    long_count = long_len.shape[1]
    short_count = short_len.shape[1]
    owners = token_owner[:, 0]
    slots = capacity * n_model
    positions = jnp.arange(group, dtype=jnp.int32)
    ranks = slot_ranks(owners, devices)
    requests = jnp.full((devices, slots), -1, jnp.int32).at[owners, ranks].set(token_row)
    received = lax.all_to_all(requests, ("dp", "mp"), split_axis=0, concat_axis=0, tiled=True)
    present = received >= 0
    looked = embed_table[jnp.where(present, received, 0)].astype(jnp.bfloat16)
    returned = lax.all_to_all(looked, ("dp", "mp"), split_axis=0, concat_axis=0, tiled=True)
    fetched = returned[owners, ranks]
    own_inputs = lax.dynamic_slice_in_dim(fetched, own_start, tok_dev)
    heads_cols = heads_weight.shape[2]
    joined = heads_weight.reshape(width, 3 * heads_cols)
    blocks = group // LONG_LEN
    segment, key_ok = row_layout(positions, long_len[0], short_len[0], half)
    seg_blocks = segment.reshape(blocks, LONG_LEN)
    allowed = (seg_blocks[:, :, None] == seg_blocks[:, None, :]) & key_ok.reshape(blocks, LONG_LEN)[
        :, None, :
    ]

    def split_heads(matrix):
        return matrix.reshape(blocks, LONG_LEN, heads_cols // HEAD, HEAD)

    projected = jnp.dot(fetched, joined, preferred_element_type=jnp.float32).astype(jnp.bfloat16)
    query = split_heads(projected[:, :heads_cols])
    key_part = split_heads(projected[:, heads_cols : 2 * heads_cols])
    value = split_heads(projected[:, 2 * heads_cols :])
    attended_full, log_total = attend(query, key_part, value, allowed)
    attended = attended_full.reshape(-1, heads_cols).astype(jnp.bfloat16)
    mixed = lax.psum_scatter(
        jnp.dot(attended, mix_weight, preferred_element_type=jnp.float32),
        "mp",
        scatter_dimension=0,
        tiled=True,
    )
    first_hidden = own_inputs.astype(jnp.float32) + mixed
    normed, first_back = jax.vjp(layer_norm, first_hidden, first_gain, first_shift)
    normed_low = normed.astype(jnp.bfloat16)
    ffn_in = lax.all_gather(normed_low, "mp", axis=0, tiled=True)
    up_pre = jnp.dot(ffn_in, up_weight, preferred_element_type=jnp.float32)
    activated_full, gelu_back = jax.vjp(exact_gelu, up_pre)
    activated = activated_full.astype(jnp.bfloat16)
    branch = lax.psum_scatter(
        jnp.dot(activated, down_weight, preferred_element_type=jnp.float32),
        "mp",
        scatter_dimension=0,
        tiled=True,
    )
    second_hidden = normed + branch
    block_rows, second_back = jax.vjp(layer_norm, second_hidden, second_gain, second_shift)
    block_out = block_rows.astype(jnp.bfloat16)
    per_short = tok_dev // SHORT_LEN
    per_long = tok_dev // LONG_LEN
    slot_ids = jnp.arange(per_short, dtype=jnp.int32)
    is_long = model_pos < n_model // 2
    stride = jnp.where(is_long, LONG_LEN, SHORT_LEN)
    limit = jnp.where(is_long, per_long, per_short)
    cls_valid = slot_ids < limit
    cls_pos = jnp.where(cls_valid, slot_ids * stride, tok_dev)
    pooled = jnp.where(cls_valid[:, None], block_rows[jnp.minimum(cls_pos, tok_dev - 1)], 0.0)
    pooled_all = lax.all_gather(pooled, ("dp", "mp"), axis=0, tiled=True)
    group_ids = np.arange(n_data)[:, None]
    long_ids = np.arange(long_count)[None, :]
    short_ids = np.arange(short_count)[None, :]
    long_order = (group_ids * n_model + long_ids // per_long) * per_short + long_ids % per_long
    short_order = (
        group_ids * n_model + n_model // 2 + short_ids // per_short
    ) * per_short + short_ids % per_short
    order = jnp.asarray(
        np.concatenate([long_order, short_order], axis=1).reshape(-1), dtype=jnp.int32
    )

    def pooled_loss(gathered):
        return ranking_loss(gathered[order], pairing)

    loss, loss_back = jax.vjp(pooled_loss, pooled_all)
    pair_count = pairing.shape[0] // 2
    (grad_pooled_all,) = loss_back(jnp.asarray(pair_count, jnp.float32))
    grad_pooled = lax.dynamic_slice_in_dim(grad_pooled_all, place * per_short, per_short, 0)
    grad_out = (
        upper_grad.astype(jnp.float32)
        .at[cls_pos]
        .add(jnp.where(cls_valid[:, None], grad_pooled, 0.0), mode="drop")
    )
    grad_second, grad_gain_two, grad_shift_two = second_back(grad_out)
    grad_branch = grad_second.astype(jnp.bfloat16)
    branch_all = lax.all_gather(grad_branch, "mp", axis=0, tiled=True)
    grad_act = jnp.dot(branch_all, down_weight.T, preferred_element_type=jnp.float32)
    grad_down = rows_product(activated, branch_all)
    (grad_pre_full,) = gelu_back(grad_act)
    grad_pre = grad_pre_full.astype(jnp.bfloat16)
    grad_up = rows_product(ffn_in, grad_pre)
    grad_normed_ffn = lax.psum_scatter(
        jnp.dot(grad_pre, up_weight.T, preferred_element_type=jnp.float32),
        "mp",
        scatter_dimension=0,
        tiled=True,
    )
    grad_first, grad_gain_one, grad_shift_one = first_back(grad_second + grad_normed_ffn)
    grad_mixed = grad_first.astype(jnp.bfloat16)
    mixed_all = lax.all_gather(grad_mixed, "mp", axis=0, tiled=True)
    grad_mix = rows_product(attended, mixed_all)
    grad_attended = jnp.dot(mixed_all, mix_weight.T, preferred_element_type=jnp.float32).astype(
        jnp.bfloat16
    )
    grad_query, grad_key, grad_value = attend_back(
        query, key_part, value, allowed, log_total, split_heads(grad_attended)
    )
    grad_proj = jnp.concatenate(
        [
            grad_query.reshape(-1, heads_cols),
            grad_key.reshape(-1, heads_cols),
            grad_value.reshape(-1, heads_cols),
        ],
        axis=1,
    ).astype(jnp.bfloat16)
    grad_heads = rows_product(fetched, grad_proj).reshape(width, 3, heads_cols)
    grad_part = jnp.dot(grad_proj, joined.T, preferred_element_type=jnp.float32)
    own_part = lax.dynamic_slice_in_dim(grad_part, own_start, tok_dev, 0) + grad_first
    grad_tokens = lax.dynamic_update_slice_in_dim(grad_part, own_part, own_start, 0)
    outgoing = jnp.zeros((devices, slots, width), jnp.float32).at[owners, ranks].set(grad_tokens)
    incoming = lax.all_to_all(
        outgoing.astype(jnp.bfloat16), ("dp", "mp"), split_axis=0, concat_axis=0, tiled=True
    ).astype(outgoing.dtype)
    flat_rows = jnp.where(present, received, table_rows).reshape(-1)
    row_sum = (
        jnp.zeros((table_rows, width), jnp.float32)
        .at[flat_rows]
        .add(incoming.reshape(-1, width), mode="drop")
    )
    hits = jnp.zeros((table_rows,), jnp.int32).at[flat_rows].add(1, mode="drop")
    uses = hits // n_model
    row_grad = row_sum / jnp.maximum(uses, 1).astype(jnp.float32)[:, None]
    first_new = 0.9 * first_moment + 0.1 * row_grad
    second_new = 0.95 * second_moment + 0.05 * row_grad * row_grad
    table_step = (
        first_new / first_fix / (jnp.sqrt(second_new / second_fix) + 1e-08) + 0.01 * embed_table
    )
    heads_grad, mix_grad, up_grad, down_grad = lax.psum(
        (grad_heads, grad_mix, grad_up, grad_down), "dp"
    )
    norm_sums = lax.psum(
        (grad_gain_one, grad_shift_one, grad_gain_two, grad_shift_two), ("dp", "mp")
    )
    return (
        loss,
        block_out,
        heads_grad,
        mix_grad,
        up_grad,
        down_grad,
        norm_sums[0],
        norm_sums[1],
        norm_sums[2],
        norm_sums[3],
        table_step,
        first_new,
        second_new,
    )


def solution(mesh):
    in_specs = (
        P("dp", None),
        P("dp"),
        P("dp", None),
        P("dp", None),
        P(),
        P(("dp", "mp"), None),
        P(("dp", "mp"), None),
        P(("dp", "mp"), None),
        P(None, None, "mp"),
        P("mp", None),
        P(None, "mp"),
        P("mp", None),
        P(),
        P(),
        P(),
        P(),
        P(("dp", "mp"), None),
    )
    out_specs = (
        P(),
        P(("dp", "mp"), None),
        P(None, None, "mp"),
        P("mp", None),
        P(None, "mp"),
        P("mp", None),
        P(),
        P(),
        P(),
        P(),
        P(("dp", "mp"), None),
        P(("dp", "mp"), None),
        P(("dp", "mp"), None),
    )
    return jax.shard_map(body, mesh=mesh, in_specs=in_specs, out_specs=out_specs, check_vma=False)
```

profile of v0, /device:TPU:0, one launch (start us, length us, event | category | flops | bytes accessed | tf_op | source)
XLA Modules:
  0.0 786.8 jit_solution(17398144964641024640)
XLA Ops:
  8.0 9.0 %reduce-window.6 = s32[32,8,128]{2,1,0:T(8,128)S(1)} reduce-window(s32[32,8,128]{2,1,0:T(8,128)S(1)} %fusion.54, s32[]{:T(128)} %constant.235.clone.1), window={size=1x1x128 pad=0_0x0_0x127_0}, to_apply=%region_0.0 | reduce-window | flops 4161536 | bytes 262148 | tf_op jit(solution)/shard_map/reduce-window
  21.0 4.5 scatter_custom_fusion.7
  25.6 14.2 %all_to_all.25 = s32[32,1,64]{2,1,0:T(1,128)S(1)} all-to-all(s32[32,1,64]{2,1,0:T(1,128)S(1)} %all_to_all.16), channel_id=1, replica_groups=mesh['dp'=8,'mp'=4] {'dp','mp'}, dimensions={0} | all-to-all | bytes 16384 | tf_op jit(solution)/shard_map/all_to_all | solution.py:145
  40.5 12.8 %gather_fusion = bf16[2048,768]{1,0:T(8,128)(2,1)} fusion(f32[2048,768]{1,0:T(8,128)} %param.23, s32[2048]{0:T(1024)S(1)} %broadcast_clamp_fusion), kind=kCustom, calls=%fused_computation | custom fusion | bytes 6299648 | tf_op jit(solution)/shard_map/gather | solution.py:147
  53.3 3.7 all-to-all-start.1
  57.7 71.1 %all-to-all-done.1 = bf16[32,64,768]{2,1,0:T(8,128)(2,1)} async-done(((bf16[32,64,768]{2,1,0:T(8,128)(2,1)}), bf16[32,64,768]{2,1,0:T(8,128)(2,1)}, u32[]{:S(2)}, u32[]{:S(2)}) %all-to-all-start.1) | async-done | bytes 3145760 | tf_op jit(solution)/shard_map/all_to_all | solution.py:148
  128.8 14.5 %gather_fusion.1 = bf16[1024,768]{1,0:T(8,128)(2,1)S(1)} fusion(bf16[32,64,768]{2,1,0:T(8,128)(2,1)} %all-to-all-done.1, s32[1024]{0:T(1024)S(1)} %bitcast.133), kind=kCustom, calls=%fused_computation.1 | custom fusion | bytes 3153920 | tf_op jit(solution)/shard_map/gather | solution.py:149
  143.3 2.8 convolution_convert_fusion
  149.2 2.3 fusion.31
  151.6 37.8 %reduce-scatter.4.cloned.1.call-done = f32[256,768]{1,0:T(8,128)} async-done(((f32[1024,768]{1,0:T(8,128)}), f32[256,768]{1,0:T(8,128)}) %reduce-scatter.4.cloned.1.call-update) | async-done | bytes 786448 | tf_op jit(solution)/shard_map/reduce_scatter | solution.py:169
  189.3 1.3 fusion.118
  190.9 0.9 fusion.25
  192.1 19.6 %all-gather.4.cloned.1.call-done = bf16[1024,768]{1,0:T(8,128)(2,1)} async-done(((bf16[256,768]{1,0:T(8,128)(2,1)}), bf16[1024,768]{1,0:T(8,128)(2,1)}) %all-gather.4.cloned.1.call-update) | async-done | bytes 1572880 | tf_op jit(solution)/shard_map/all_gather | solution.py:178
  211.7 10.4 %multiply_convert_fusion = (bf16[1024,768]{1,0:T(8,128)(2,1)S(1)}, f32[1024,768]{1,0:T(8,128)}, f32[1024,768]{1,0:T(8,128)}) fusion(bf16[1024,768]{1,0:T(8,128)(2,1)} %all-gather.4.cloned.1.call-done, bf16[768,768]{1,0:T(8,128)(2,1)S(1)} %copy-done), kind=kOutput, calls=%fused_computation.29 | convolution fusion | flops 1259077632 | bytes 10616832 | tf_op jit(solution)/shard_map/dot_general | solution.py:179
  222.1 1.1 copy-done.61
  223.2 4.3 fusion.120
  228.6 0.9 convert_element_type.76
  233.0 32.7 %reduce-scatter.6.cloned.1.call-done = f32[256,768]{1,0:T(8,128)} async-done(((f32[1024,768]{1,0:T(8,128)}), f32[256,768]{1,0:T(8,128)}) %reduce-scatter.6.cloned.1.call-update) | async-done | bytes 786448 | tf_op jit(solution)/shard_map/reduce_scatter | solution.py:182
  265.7 1.4 fusion.115
  268.0 1.7 fusion.114
  269.7 1.3 gather_fusion.2
  271.8 42.6 %all_gather.13 = f32[256,768]{1,0:T(8,128)S(1)} all-gather(f32[8,768]{1,0:T(8,128)S(1)} %broadcast_select_fusion), channel_id=1, replica_groups=mesh['dp'=8,'mp'=4] {'dp','mp'}, dimensions={0}, use_global_device_ids=true | all-gather | bytes 811008 | tf_op jit(solution)/shard_map/all_gather | solution.py:200
  314.4 1.8 gather_fusion.3
  316.2 1.1 multiply_reduce_fusion.8
  317.4 1.1 broadcast_multiply_fusion
  319.3 1.5 gather_fusion.4
  320.9 1.5 fusion.110
  323.9 2.2 gather_fusion.6
  326.9 1.3 subtract_reduce_fusion
  329.0 4.7 scatter_fusion
  333.7 2.0 fusion.55
  335.7 2.1 fusion.57
  337.8 2.3 scatter_custom_fusion.1
  340.0 2.7 scatter_custom_fusion.2
  342.7 1.3 multiply_reduce_fusion.7
  344.1 3.3 scatter_custom_fusion.3
  347.4 2.9 scatter_custom_fusion.4
  350.2 2.0 multiply_reduce_fusion.1
  352.3 1.5 fusion.113
  354.7 15.9 %all-gather.6.cloned.1.call-done = bf16[1024,768]{1,0:T(8,128)(2,1)} async-done(((bf16[256,768]{1,0:T(8,128)(2,1)}), bf16[1024,768]{1,0:T(8,128)(2,1)}) %all-gather.6.cloned.1.call-update) | async-done | bytes 1572880 | tf_op jit(solution)/shard_map/all_gather | solution.py:226
  370.6 5.6 add_convert_fusion
  376.3 1.1 copy-done.62
  377.4 3.1 fusion.121
  380.6 38.1 %reduce-scatter.8.cloned.1.call-done = f32[256,768]{1,0:T(8,128)} async-done(((f32[1024,768]{1,0:T(8,128)}), f32[256,768]{1,0:T(8,128)}) %reduce-scatter.8.cloned.1.call-update) | async-done | bytes 786448 | tf_op jit(solution)/shard_map/reduce_scatter | solution.py:232
  418.6 2.1 multiply_reduce_fusion.2
  423.3 4.7 fusion.123
  428.1 14.3 %all-gather.8.cloned.1.call-done = bf16[1024,768]{1,0:T(8,128)(2,1)} async-done(((bf16[256,768]{1,0:T(8,128)(2,1)}), bf16[1024,768]{1,0:T(8,128)(2,1)}) %all-gather.8.cloned.1.call-update) | async-done | bytes 1572880 | tf_op jit(solution)/shard_map/all_gather | solution.py:240
  442.4 2.1 fusion.15
  448.3 3.1 fusion.124
  451.4 2.2 add_dynamic-update-slice_fusion
  453.6 8.7 %scatter_custom_fusion.8 = f32[2048,768]{1,0:T(8,128)} fusion(s32[1024]{0:T(1024)} %copy-done.50, f32[1024,768]{1,0:T(8,128)} %add_dynamic-update-slice_fusion, f32[]{:T(128)} %constant.253.clone.1), kind=kCustom, calls=%fused_computation.25 | custom fusion | bytes 6291968
  462.3 4.8 convert_element_type.85
  467.0 4.7 all-to-all-start.2
  472.0 4.9 fusion.122
  476.9 1.3 fusion.29
  478.2 2.3 fusion.125
  482.0 11.3 %scatter_custom_fusion.6 = s32[2048]{0:T(1024)S(1)} fusion(s32[2048]{0:T(1024)S(1)} %bitcast.156, s32[2048]{0:T(1024)S(1)} %broadcast.829, s32[]{:T(128)} %constant.235.clone.1), kind=kCustom, calls=%fused_computation.198 | custom fusion | flops 2048 | bytes 8196 | tf_op jit(solution)/shard_map/scatter-add | solution.py:270
  494.7 135.3 %all-reduce = (f32[768]{0:T(1024)}, f32[768]{0:T(1024)}, f32[768]{0:T(1024)}, f32[768]{0:T(1024)}) all-reduce(f32[768]{0:T(1024)S(1)} %copy-done.37, f32[768]{0:T(1024)S(1)} %copy-done.38, f32[768]{0:T(1024)S(1)} %copy-done.35, f32[768]{0:T(1024)S(1)} %copy-done.36), channel_id=1, replica_groups=mesh['dp'=8,'mp'=4] {'dp','mp'}, use_global_device_ids=true, to_apply=%region_38.39 | all-reduce | flops 3072 | bytes 24576 | tf_op jit(solution)/shard_map/psum | solution.py:281
  629.9 17.7 %scatter_custom_fusion.5 = f32[2048,768]{1,0:T(8,128)} fusion(s32[2048]{0:T(1024)S(1)} %bitcast.157, bf16[2048,768]{1,0:T(8,128)(2,1)} %bitcast.25, f32[]{:T(128)} %constant.253.clone.1), kind=kCustom, calls=%fused_computation.18 | custom fusion | flops 3145728 | bytes 9437188 | tf_op jit(solution)/shard_map/scatter-add | solution.py:268
  647.6 17.2 %multiply_add_fusion = (f32[2048,768]{1,0:T(8,128)}, f32[2048,768]{1,0:T(8,128)}, f32[2048,768]{1,0:T(8,128)}) fusion(f32[2048,768]{1,0:T(8,128)} %param.23, f32[2048,768]{1,0:T(8,128)} %scatter_custom_fusion.5, f32[2048]{0:T(1024)S(1)} %fusion.70, f32[2048,768]{1,0:T(8,128)} %param.24, f32[2048,768]{1,0:T(8,128)} %param.25), kind=kLoop, calls=%fused_computation.20 | loop fusion | flops 22020096 | bytes 44048384 | tf_op jit(solution)/shard_map/add | solution.py:276
  664.8 107.3 %all-reduce.4.cloned.1.call-done = (f32[768,3,192]{0,2,1:T(8,128)}, f32[192,768]{1,0:T(8,128)}, f32[768,768]{1,0:T(8,128)}, f32[768,768]{1,0:T(8,128)}) async-done(((f32[768,3,192]{0,2,1:T(8,128)}, f32[192,768]{1,0:T(8,128)}, f32[768,768]{1,0:T(8,128)}, f32[768,768]{1,0:T(8,128)}), (f32[768,3,192]{0,2,1:T(8,128)}, f32[192,768]{1,0:T(8,128)}, f32[768,768]{1,0:T(8,128)}, ...) | async-done | bytes 7077904 | tf_op jit(solution)/shard_map/psum | solution.py:278
  772.0 2.9 copy.137
  775.8 1.4 copy.139
  777.2 1.4 copy.140
  (224 shorter events, 29.4 us)
Async XLA Ops:
  7.2 204.5 %copy-start = (bf16[768,768]{1,0:T(8,128)(2,1)S(1)}, bf16[768,768]{1,0:T(8,128)(2,1)}, u32[]{:S(2)}) copy-start(bf16[768,768]{1,0:T(8,128)(2,1)} %param.28) | copy-start | bytes 3538948
  53.3 3.8 copy-start.57
  53.3 3.9 copy-start.58
  53.3 75.5 %all-to-all-start.1 = ((bf16[32,64,768]{2,1,0:T(8,128)(2,1)}), bf16[32,64,768]{2,1,0:T(8,128)(2,1)}, u32[]{:S(2)}, u32[]{:S(2)}) async-start(bf16[32,64,768]{2,1,0:T(8,128)(2,1)} %bitcast.134), calls=%async_computation.1 | async-start | bytes 6291456 | tf_op jit(solution)/shard_map/all_to_all | solution.py:148
  57.0 132.3 %reduce-scatter.4.cloned.1.call-start = ((), (), s32[]{:S(2)}) async-start(), calls=%async_computation.6 | async-start | bytes 3932160 | tf_op jit(solution)/shard_map/reduce_scatter | solution.py:169
  143.3 46.0 %copy-start.7 = (bf16[1024,768]{1,0:T(8,128)(2,1)}, bf16[1024,768]{1,0:T(8,128)(2,1)S(1)}, u32[]{:S(2)}) copy-start(bf16[1024,768]{1,0:T(8,128)(2,1)S(1)} %gather_fusion.1) | copy-start | bytes 4718596
  146.4 1.4 copy-start.16
  146.4 1.3 copy-start.12
  146.5 1.3 copy-start.14
  147.0 1.1 copy-start.1
  147.0 1.1 copy-start.26
  147.3 0.8 copy-start.27
  147.3 1.8 copy-start.18
  151.5 39.4 %copy-start.25 = (f32[768]{0:T(1024)S(1)}, f32[768]{0:T(1024)}, u32[]{:S(2)}) copy-start(f32[768]{0:T(1024)} %param.30) | copy-start | bytes 9220
  151.5 39.4 %copy-start.33 = (f32[768]{0:T(1024)S(1)}, f32[768]{0:T(1024)}, u32[]{:S(2)}) copy-start(f32[768]{0:T(1024)} %param.31) | copy-start | bytes 9220
  151.5 60.2 %all-gather.4.cloned.1.call-start = ((), (), s32[]{:S(2)}) async-start(), calls=%async_computation.7 | async-start | bytes 1966080 | tf_op jit(solution)/shard_map/all_gather | solution.py:178
  190.8 31.2 %copy-start.41 = (f32[256]{0:T(256)}, f32[256]{0:T(256)S(1)}, u32[]{:S(2)}) copy-start(f32[256]{0:T(256)S(1)} %multiply_reduce_fusion.6) | copy-start | bytes 3076
  190.9 74.8 %copy-start.29 = (f32[256]{0:T(256)}, f32[256]{0:T(256)S(1)}, u32[]{:S(2)}) copy-start(f32[256]{0:T(256)S(1)} %fusion.97) | copy-start | bytes 3076
  191.9 73.8 %reduce-scatter.6.cloned.1.call-start = ((), (), s32[]{:S(2)}) async-start(), calls=%async_computation.8 | async-start | bytes 3932160 | tf_op jit(solution)/shard_map/reduce_scatter | solution.py:182
  222.1 1.1 copy-start.61
  227.6 1.0 copy-start.20
  227.6 4.8 copy-start.56
  227.6 38.1 %copy-start.34 = (f32[768]{0:T(1024)S(1)}, f32[768]{0:T(1024)}, u32[]{:S(2)}) copy-start(f32[768]{0:T(1024)} %param.31) | copy-start | bytes 9220
  227.6 143.0 %all-gather.6.cloned.1.call-start = ((), (), s32[]{:S(2)}) async-start(), calls=%async_computation.9 | async-start | bytes 1966080 | tf_op jit(solution)/shard_map/all_gather | solution.py:226
  231.2 1.8 copy-start.52
  231.2 36.2 %copy-start.53 = (s32[80]{0:T(128)}, s32[80]{0:T(128)S(1)}, u32[]{:S(2)}) copy-start(s32[80]{0:T(128)S(1)} %get-tuple-element.69) | copy-start | bytes 964
  267.2 0.8 copy-start.31
  268.0 1.7 copy-start.39
  317.3 8.8 %copy-start.45 = (f32[160]{0:T(256)}, f32[160]{0:T(256)S(1)}, u32[]{:S(2)}) copy-start(f32[160]{0:T(256)S(1)} %multiply_reduce_fusion.8) | copy-start | bytes 1924
  319.3 8.9 %copy-start.11 = (f32[80,768]{1,0:T(8,128)}, f32[80,768]{1,0:T(8,128)S(1)}, u32[]{:S(2)}) copy-start(f32[80,768]{1,0:T(8,128)S(1)} %gather_fusion.5) | copy-start | bytes 737284
  320.9 21.8 %copy-start.3 = (f32[160,768]{1,0:T(8,128)S(1)}, f32[160,768]{1,0:T(8,128)}, u32[]{:S(2)}) copy-start(f32[160,768]{1,0:T(8,128)} %gather_fusion.3) | copy-start | bytes 1474564
  322.4 1.0 copy-start.55
  328.3 15.8 %copy-start.46 = (f32[160]{0:T(256)S(1)}, f32[160]{0:T(256)}, u32[]{:S(2)}) copy-start(f32[160]{0:T(256)} %copy-done.45) | copy-start | bytes 1924
  333.7 13.6 %copy-start.51 = (pred[8]{0:T(512)(128)(4,1)S(1)}, pred[8]{0:T(512)(128)(4,1)}, u32[]{:S(2)}) copy-start(pred[8]{0:T(512)(128)(4,1)} %iota_compare_fusion.5) | copy-start | bytes 28
  335.7 14.5 %copy-start.28 = (f32[768]{0:T(1024)S(1)}, f32[768]{0:T(1024)}, u32[]{:S(2)}) copy-start(f32[768]{0:T(1024)} %param.32) | copy-start | bytes 9220
  335.7 14.5 %copy-start.32 = (f32[256]{0:T(256)S(1)}, f32[256]{0:T(256)}, u32[]{:S(2)}) copy-start(f32[256]{0:T(256)} %copy-done.31) | copy-start | bytes 3076
  335.7 14.5 %copy-start.40 = (f32[256]{0:T(256)S(1)}, f32[256]{0:T(256)}, u32[]{:S(2)}) copy-start(f32[256]{0:T(256)} %copy-done.39) | copy-start | bytes 3076
  342.7 9.6 %copy-start.44 = (f32[256]{0:T(256)S(1)}, f32[256]{0:T(256)}, u32[]{:S(2)}) copy-start(f32[256]{0:T(256)} %copy-done.43) | copy-start | bytes 3076
  353.8 22.5 %copy-start.49 = (f32[256]{0:T(256)}, f32[256]{0:T(256)S(1)}, u32[]{:S(2)}) copy-start(f32[256]{0:T(256)S(1)} %negate_multiply_fusion.2) | copy-start | bytes 3076
  354.7 64.0 %reduce-scatter.8.cloned.1.call-start = ((), (), s32[]{:S(2)}) async-start(), calls=%async_computation.10 | async-start | bytes 3932160 | tf_op jit(solution)/shard_map/reduce_scatter | solution.py:232
  376.3 1.1 copy-start.62
  380.5 38.1 %copy-start.30 = (f32[256]{0:T(256)S(1)}, f32[256]{0:T(256)}, u32[]{:S(2)}) copy-start(f32[256]{0:T(256)} %copy-done.29) | copy-start | bytes 3076
  380.5 40.3 %copy-start.42 = (f32[256]{0:T(256)S(1)}, f32[256]{0:T(256)}, u32[]{:S(2)}) copy-start(f32[256]{0:T(256)} %copy-done.41) | copy-start | bytes 3076
  380.5 61.9 %all-gather.8.cloned.1.call-start = ((), (), s32[]{:S(2)}) async-start(), calls=%async_computation.11 | async-start | bytes 1966080 | tf_op jit(solution)/shard_map/all_gather | solution.py:240
  428.1 16.6 %copy-start.2 = (f32[8,3,128,128]{2,3,1,0:T(8,128)S(1)}, f32[8,3,128,128]{2,3,1,0:T(8,128)}, u32[]{:S(2)}) copy-start(f32[8,3,128,128]{2,3,1,0:T(8,128)} %copy-done.1) | copy-start | bytes 4718596
  442.4 2.9 copy-start.17
  445.3 1.0 copy-start.15
  445.9 1.1 copy-start.13
  446.9 1.3 copy-start.59
  448.3 3.1 copy-start.23
  448.3 3.1 copy-start.48
  467.0 162.9 %all-to-all-start.2 = ((bf16[32,64,768]{2,1,0:T(8,128)(2,1)}), bf16[32,64,768]{2,1,0:T(8,128)(2,1)}, u32[]{:S(2)}, u32[]{:S(2)}) async-start(bf16[32,64,768]{2,1,0:T(8,128)(2,1)} %bitcast.135), calls=%async_computation.5 | async-start | bytes 6291456 | tf_op jit(solution)/shard_map/all_to_all | solution.py:261
  471.8 5.1 copy-start.4
  471.8 5.1 copy-start.6
  471.8 300.3 %all-reduce.4.cloned.1.call-start = ((), (), s32[]{:S(2)}) async-start(), calls=%async_computation.12 | async-start | bytes 14155776 | tf_op jit(solution)/shard_map/psum | solution.py:278
  472.0 6.2 copy-start.8
  472.0 6.2 copy-start.24
  480.5 14.1 %copy-start.35 = (f32[768]{0:T(1024)S(1)}, f32[768]{0:T(1024)}, u32[]{:S(2)}) copy-start(f32[768]{0:T(1024)} %get-tuple-element.19) | copy-start | bytes 9220
  480.5 14.1 %copy-start.36 = (f32[768]{0:T(1024)S(1)}, f32[768]{0:T(1024)}, u32[]{:S(2)}) copy-start(f32[768]{0:T(1024)} %get-tuple-element.23) | copy-start | bytes 9220
  480.5 14.2 %copy-start.37 = (f32[768]{0:T(1024)S(1)}, f32[768]{0:T(1024)}, u32[]{:S(2)}) copy-start(f32[768]{0:T(1024)} %get-tuple-element.21) | copy-start | bytes 9220
  480.5 14.2 %copy-start.38 = (f32[768]{0:T(1024)S(1)}, f32[768]{0:T(1024)}, u32[]{:S(2)}) copy-start(f32[768]{0:T(1024)} %get-tuple-element.24) | copy-start | bytes 9220
  772.0 3.0 copy-start.19
  772.0 3.8 copy-start.10
  775.0 2.2 copy-start.9
  (8 other events, 5.0 us)
Sparse Core Ops, SparseCore 0:
  151.6 37.6 reduce-scatter.3
  192.0 19.6 all-gather.3
  227.7 37.9 reduce-scatter.5
  354.8 15.7 all-gather.5
  380.6 37.9 reduce-scatter.7
  422.7 19.6 all-gather.7
  480.7 291.3 all-reduce.3
where the time goes:
time: 794 us; the launch traced here: 787 us
  waiting for transfers between devices  337 us (42%)
  blocking collectives  192 us (24%)
  other arithmetic  111 us (14%)
  local copies, waits for them, and re-layouts  64.9 us (8%)
  matrix products  55.6 us (7%)
  between operations  17.6 us (2%)
  starting transfers between devices  9.01 us (1%)
    psum x1, blocking collectives, body(): lax.psum((grad_gain_one, grad_shift_one, grad_gain_two, grad_shift_two),...  135 us
    psum x1, waiting for transfers between devices, body(): lax.psum((grad_heads, grad_mix, grad_up, grad_down), 'dp')  107 us
    all_to_all x1, waiting for transfers between devices, body(): lax.all_to_all(looked, ('dp', 'mp'), split_axis=0, concat_axis=0, tiled=T...  71.1 us
    all_gather x1, blocking collectives, body(): pooled_all = lax.all_gather(pooled, ('dp', 'mp'), axis=0, tiled=True)  42.6 us
    reduce_scatter x1, waiting for transfers between devices, body(): lax.psum_scatter(jnp.dot(grad_pre, up_weight.T, preferred_element_type=jn...  38.1 us
    reduce_scatter x1, waiting for transfers between devices, body(): lax.psum_scatter(jnp.dot(attended, mix_weight, preferred_element_type=jnp...  37.8 us
    reduce_scatter x1, waiting for transfers between devices, body(): lax.psum_scatter(jnp.dot(activated, down_weight, preferred_element_type=j...  32.7 us
    unnamed x139, local copies, waits for them, and re-layouts  27.4 us
  transfers between devices with their start and end apart: 9, of which 8 were waited for; matrix products, arithmetic and copies ran while one was open for 8% of the time, Pallas kernels for 0%

commit v1 on v0

v1 whole, which is shorter than its diff:
```python
import functools
from types import SimpleNamespace

import jax
import jax.numpy as jnp
from jax import lax
from jax.experimental import pallas as pl
from jax.experimental.pallas import tpu as pltpu
from jax.sharding import PartitionSpec as P

HEAD = 64
LONG_LEN = 128
SHORT_LEN = 32
BLOCK = 128
SLOTS = 16
MESH = pl.DeviceIdType.MESH
bf16 = jnp.bfloat16
f32 = jnp.float32
i32 = jnp.int32

first_fix = 1.0 - 0.9**10
second_fix = 1.0 - 0.95**10


def nn(left, right):
    return lax.dot_general(left, right, (((1,), (0,)), ((), ())), preferred_element_type=f32)


def nt(left, right):
    return lax.dot_general(left, right, (((1,), (1,)), ((), ())), preferred_element_type=f32)


def tn(left, right):
    return lax.dot_general(left, right, (((0,), (0,)), ((), ())), preferred_element_type=f32)


def iota(shape, axis):
    return lax.broadcasted_iota(i32, shape, axis)


def column_of(row):
    count = row.shape[1]
    eye = iota((count, count), 0) == iota((count, count), 1)
    return jnp.sum(jnp.where(eye, row, 0.0), axis=1, keepdims=True)


def mean_of(values):
    return jnp.mean(values, axis=-1, keepdims=True)


def norm_forward(hidden):
    centered = hidden - mean_of(hidden)
    scale = lax.rsqrt(mean_of(centered * centered) + 1e-12)
    return centered * scale, scale


def norm_back(grad, normal, scale, gain):
    scaled = grad * gain
    return scale * (scaled - mean_of(scaled) - normal * mean_of(scaled * normal))


class Net:
    def __init__(self, send_sems, recv_sems):
        self.send_sems, self.recv_sems = send_sems, recv_sems
        self.count = 0
        self.open = []

    def send(self, src, dst, device):
        at = self.count
        self.count += 1
        copy = pltpu.make_async_remote_copy(
            src_ref=src,
            dst_ref=dst,
            send_sem=self.send_sems.at[at],
            recv_sem=self.recv_sems.at[at],
            device_id=device,
            device_id_type=MESH,
        )
        copy.start()
        self.open.append(copy)
        return copy

    def sent(self, copy):
        copy.wait_send()
        self.open = [item for item in self.open if item is not copy]

    def drain(self):
        for copy in self.open:
            copy.wait_send()
        self.open = []


class Reduce:
    def __init__(self, net, part, whole, land, place, bits):
        self.net, self.part, self.whole, self.land = net, part, whole, land
        self.data_pos, self.model_pos = place
        self.bits = bits
        rows, width = part.shape
        self.half = width // 2
        self.row, self.len = 0, rows
        self.offset = 0
        self.stage = 0
        self.halved = []
        grows = sum(1 for stage in range(len(bits)) if self.halves(stage))
        self.todo = [self.add] * len(bits) + [self.grow] * grows

    def step(self):
        self.todo.pop(0)()

    def halves(self, stage):
        return stage == 0 or (self.part.shape[0] >> (stage - 1)) % 32 == 0

    def partner(self, bit):
        mine = lax.rem(lax.div(self.data_pos, 1 << bit), 2)
        return mine, (self.data_pos + (1 - 2 * mine) * (1 << bit), self.model_pos)

    def start(self):
        mine, device = self.partner(self.bits[self.stage])
        halved = self.halves(self.stage)
        count = self.len
        if self.stage == 0:
            away = pl.multiple_of((1 - mine) * self.half, 128)
            self.col = pl.multiple_of(mine * self.half, 128)
            src = self.part.at[:, pl.ds(away, self.half)]
        else:
            away = self.row
            if halved:
                count = self.len // 2
                away = pl.multiple_of(self.row + (1 - mine) * count, 16)
                self.row = pl.multiple_of(self.row + mine * count, 16)
                self.len = count
            src = self.part.at[pl.ds(away, count), pl.ds(self.col, self.half)]
        self.halved.append(halved)
        self.now = self.land.at[pl.ds(self.offset, count)]
        self.offset += count
        self.copy = self.net.send(src, self.now, device)

    def add(self):
        self.copy.wait_recv()
        last = self.stage == len(self.bits) - 1
        if not self.halved[-1]:
            self.net.sent(self.copy)
        target = self.whole if last else self.part
        cols = pl.ds(self.col, self.half)
        step = 48
        now, row, part = self.now, self.row, self.part

        def tile(at, carry):
            here = pl.multiple_of(at * step, 16)
            there = pl.ds(pl.multiple_of(row + here, 16), step)
            total = part[there, cols].astype(f32) + now[pl.ds(here, step), :].astype(f32)
            target[there, cols] = total.astype(bf16)
            return carry

        lax.fori_loop(0, self.len // step, tile, 0)
        if last:
            self.spread()
        else:
            self.stage += 1
            self.start()

    def spread(self):
        while self.stage and not self.halved[self.stage]:
            self.stage -= 1
        _, device = self.partner(self.bits[self.stage])
        rows = pl.ds(self.row, self.len) if self.stage else slice(None)
        here = self.whole.at[rows, pl.ds(self.col, self.half)]
        self.copy = self.net.send(here, here, device)

    def grow(self):
        self.copy.wait_recv()
        if self.stage == 0:
            return
        mine, _ = self.partner(self.bits[self.stage])
        self.row = pl.multiple_of(self.row - mine * self.len, 16)
        self.len *= 2
        self.stage -= 1
        self.spread()


def layer_kernel(
    dims,
    owner_ref,
    rowid_ref,
    long_ref,
    short_ref,
    pairing_ref,
    gain_one_ref,
    shift_one_ref,
    gain_two_ref,
    shift_two_ref,
    table_hbm,
    heads_hbm,
    mix_hbm,
    up_hbm,
    down_hbm,
    upper_hbm,
    block_out,
    weight_out,
    norm_out,
    loss_out,
    incoming_out,
    ids_out,
    *scratch,
):
    n_data, n_model = dims.n_data, dims.n_model
    s = SimpleNamespace(**dict(zip(dims.names, scratch, strict=True)))
    group_rows = dims.tok * n_model
    s.partial = s.stage
    s.gproj = s.table.at[pl.ds(0, group_rows)]
    s.gp = s.table.at[pl.ds(group_rows, group_rows)]
    s.outgoing = s.found
    s.incoming = s.returned
    tok, width, cols, pad, ff = dims.tok, dims.width, dims.cols, dims.pad, dims.ff
    devices = n_data * n_model
    group = tok * n_model
    chunks = tok // BLOCK
    span = BLOCK * n_model
    slots = devices * SLOTS
    table_rows = table_hbm.shape[0]
    d = lax.axis_index("dp")
    m = lax.axis_index("mp")
    me = d * n_model + m
    core = lax.rem(m, 2)
    side = lax.div(m, 2)
    m1 = m + 1 - 2 * core
    m2 = m + 2 - 4 * side
    m3 = m1 + m2 - m
    by_core = (d, m1)
    by_side = (d, m2)
    net = Net(s.send_sems, s.recv_sems)

    def at_device(place):
        return (lax.div(place, n_model), lax.rem(place, n_model))

    def other(j):
        return lax.rem(me + j, devices)

    barrier = pltpu.get_barrier_semaphore()

    def greet(j, carry):
        pl.semaphore_signal(barrier, inc=1, device_id=at_device(other(j)), device_id_type=MESH)
        return carry

    lax.fori_loop(1, devices, greet, 0)

    stage_rows = s.stage.shape[1]
    table_parts = table_rows // stage_rows

    def table_copy(at):
        return pltpu.make_async_copy(
            table_hbm.at[pl.ds(at * stage_rows, stage_rows)],
            s.stage.at[at % 2],
            s.load_sems.at[at % 2],
        )

    table_copy(0).start()
    table_copy(1).start()
    loads = []

    def load(src, dst):
        copy = pltpu.make_async_copy(src, dst, s.load_sems.at[2 + len(loads)])
        copy.start()
        loads.append(copy)

    wt, mixw, upw, downw = s.wt, s.mixw, s.upw, s.downw
    for part in range(3):
        load(heads_hbm.at[pl.ds(part * cols, cols)], wt.at[pl.ds(part * pad, cols)])
        wt[pl.ds(part * pad + cols, pad - cols), :] = jnp.zeros((pad - cols, width), bf16)
    load(mix_hbm, mixw.at[pl.ds(0, cols)])
    mixw[pl.ds(cols, pad - cols), :] = jnp.zeros((pad - cols, width), bf16)
    load(up_hbm, upw)
    load(down_hbm, downw)
    load(upper_hbm, s.upper)

    own_at = pl.multiple_of(m * tok, 128)
    owner_row = owner_ref[:, pl.ds(own_at, tok)]
    rowid_row = rowid_ref[:, pl.ds(own_at, tok)]
    owned = iota((devices, tok), 0) == owner_row
    before = (iota((tok, tok), 0) < iota((tok, tok), 1)).astype(f32).astype(bf16)
    counted = nn(owned.astype(f32).astype(bf16), before)
    rank_row = jnp.sum(jnp.where(owned, counted, 0.0), axis=0, keepdims=True)
    slot_row = owner_row.astype(f32) * SLOTS + rank_row
    slot_row_int = slot_row.astype(i32)
    wanted_row = (rowid_row + 1).astype(f32)
    step = min(slots, 256)

    def place_slots(at, carry):
        here = pl.ds(pl.multiple_of(at * step, step), step)
        placed = iota((step, tok), 0) + at * step == slot_row_int
        wanted = jnp.sum(jnp.where(placed, wanted_row, 0.0), axis=1, keepdims=True)
        high = jnp.floor(wanted * (1.0 / 64.0))
        low = wanted - 64.0 * high
        s.ask[here, :] = jnp.where(iota((step, 128), 1) < 64, high, low).astype(bf16)
        s.place[here, :] = placed.astype(f32).astype(bf16)
        return carry

    lax.fori_loop(0, slots // step, place_slots, 0)
    slot_col = column_of(slot_row).astype(i32)
    s.pick[...] = (iota((tok, slots), 1) == slot_col).astype(f32).astype(bf16)

    pl.semaphore_wait(barrier, devices - 1)

    def slot_rows(place):
        return pl.ds(pl.multiple_of(place * SLOTS, SLOTS), SLOTS)

    def swap_copy(src, dst, sems, to):
        send_sems, recv_sems = sems
        return pltpu.make_async_remote_copy(
            src_ref=src.at[slot_rows(to)],
            dst_ref=dst.at[slot_rows(me)],
            send_sem=send_sems.at[to],
            recv_sem=recv_sems.at[me],
            device_id=at_device(to),
            device_id_type=MESH,
        )

    def arrival(dst, sems, place):
        send_sems, recv_sems = sems
        return pltpu.make_async_remote_copy(
            src_ref=dst.at[slot_rows(place)],
            dst_ref=dst.at[slot_rows(place)],
            send_sem=send_sems.at[place],
            recv_sem=recv_sems.at[place],
            device_id=at_device(place),
            device_id_type=MESH,
        )

    def swap_start(src, dst, sems):
        def one(j, carry):
            swap_copy(src, dst, sems, other(j)).start()
            return carry

        lax.fori_loop(1, devices, one, 0)
        dst[slot_rows(me), :] = src[slot_rows(me), :]

    def swap_arrived(dst, sems):
        def one(j, carry):
            arrival(dst, sems, other(j)).wait_recv()
            return carry

        lax.fori_loop(1, devices, one, 0)

    def swap_sent(dst, sems):
        def one(j, carry):
            arrival(dst, sems, other(j)).wait_send()
            return carry

        lax.fori_loop(1, devices, one, 0)

    ask_sems = (s.ask_send, s.ask_recv)
    row_sems = (s.row_send, s.row_recv)
    out_sems = (s.out_send, s.out_recv)
    swap_start(s.ask, s.asked, ask_sems)
    for at in range(table_parts):
        table_copy(at).wait()
        s.table[pl.ds(at * stage_rows, stage_rows), :] = s.stage[at % 2].astype(bf16)
        if at + 2 < table_parts:
            table_copy(at + 2).start()
    swap_arrived(s.asked, ask_sems)

    per_block = BLOCK // SLOTS

    def look(at, carry):
        block = lax.rem(lax.div(me, per_block) + at, slots // BLOCK)
        rows = pl.ds(pl.multiple_of(block * BLOCK, BLOCK), BLOCK)
        asked = s.asked[rows, :].astype(f32)
        ident = asked[:, 0:1] * 64.0 + asked[:, 64:65] - 1.0
        eye = iota((BLOCK, BLOCK), 0) == iota((BLOCK, BLOCK), 1)
        ident_row = jnp.sum(jnp.where(eye, ident, 0.0), axis=0, keepdims=True)
        ids_out[:, rows] = jnp.broadcast_to(ident_row.astype(i32), (8, BLOCK))
        hot = (iota((BLOCK, table_rows), 1) == ident.astype(i32)).astype(f32).astype(bf16)
        s.found[rows, :] = nn(hot, s.table[...]).astype(bf16)

        def one(i, inner):
            to = block * per_block + lax.rem(lax.rem(me, per_block) + i, per_block)

            @pl.when(to != me)
            def _():
                swap_copy(s.found, s.returned, row_sems, to).start()

            return inner

        lax.fori_loop(0, per_block, one, 0)
        return carry

    lax.fori_loop(0, slots // BLOCK, look, 0)
    s.returned[slot_rows(me), :] = s.found[slot_rows(me), :]
    for copy in loads:
        copy.wait()
    swap_arrived(s.returned, row_sems)

    def rows_of(model, k):
        return pl.ds(pl.multiple_of(k * span + model * BLOCK, BLOCK), BLOCK)

    def own_rows(k):
        return pl.ds(k * BLOCK, BLOCK)

    class Gather:
        def __init__(self, buffer, k):
            self.buffer, self.k = buffer, k
            mine = buffer.at[rows_of(m, k)]
            self.far = net.send(mine, mine, by_side)
            self.near = net.send(mine, mine, by_core)

        def forward(self):
            self.far.wait_recv()
            there = self.buffer.at[rows_of(m2, self.k)]
            self.passed = net.send(there, there, by_core)

        def finish(self):
            self.near.wait_recv()
            self.passed.wait_recv()

    class Scatter:
        last = {}

        def __init__(self, k):
            self.k = k
            for copy in Scatter.last.get(k, []):
                net.sent(copy)
            part = s.partial.at[k]
            self.near = []
            for r, model in ((0, m3), (1, m1)):
                here = pl.ds(pl.multiple_of(model * BLOCK, BLOCK), BLOCK)
                s.near_send[k, r] = part[here, :].astype(bf16)
                self.near.append(
                    net.send(s.near_send.at[k, r], s.near_land.at[k, r], by_core)
                )

        def middle(self):
            k = self.k
            self.near[0].wait_recv()
            here = pl.ds(pl.multiple_of(m2 * BLOCK, BLOCK), BLOCK)
            total = s.partial[k, here, :] + s.near_land[k, 0].astype(f32)
            s.far_send[k] = total.astype(bf16)
            self.far = net.send(s.far_send.at[k], s.far_land.at[k], by_side)
            Scatter.last[k] = self.near + [self.far]

        def end(self):
            k = self.k
            self.near[1].wait_recv()
            here = pl.ds(pl.multiple_of(m * BLOCK, BLOCK), BLOCK)
            total = s.partial[k, here, :] + s.near_land[k, 1].astype(f32)
            self.far.wait_recv()
            return total + s.far_land[k].astype(f32)

    def tiles(total, step, fn):
        def one(at, carry):
            fn(pl.multiple_of(at * step, step))
            return carry

        lax.fori_loop(0, total // step, one, 0)

    x, proj, att, probs = s.x, s.proj, s.att, s.probs
    gathers = []
    for k in range(chunks):
        own = nn(s.pick[own_rows(k), :], s.returned[...])
        x[rows_of(m, k), :] = own.astype(bf16)
        gathers.append(Gather(x, k))

    lane = iota((BLOCK, BLOCK), 1)
    sub = iota((BLOCK, BLOCK), 0)
    first_half = lane < HEAD
    head_masks = [
        (lane < HEAD).astype(f32).astype(bf16),
        (lane >= HEAD).astype(f32).astype(bf16),
    ]
    heads = cols // HEAD
    long_blocks = n_model // 2
    per_long = tok // LONG_LEN
    per_short = tok // SHORT_LEN
    short_in_block = BLOCK // SHORT_LEN

    def key_mask(model, k, is_long):
        if is_long:
            return lane < long_ref[0, model * per_long + k]
        keep = None
        for j in range(short_in_block):
            size = short_ref[0, (model - long_blocks) * per_short + k * short_in_block + j]
            start = j * SHORT_LEN
            ok = (lane >= start) & (lane < start + size) & (sub >= start) & (sub < start + SHORT_LEN)
            keep = ok if keep is None else keep | ok
        return keep

    def head_parts(source, rows, h, part):
        g = h // 2
        return source[rows, pl.ds(part * pad + g * BLOCK, BLOCK)]

    def attend(k):
        def project(at):
            rows = pl.ds(pl.multiple_of(k * span + at, 256), 256)
            proj[rows, :] = nt(x[rows, :], wt[...]).astype(bf16)

        tiles(span, 256, project)

        def block(is_long, model):
            rows = rows_of(model, k)
            keep = key_mask(model, k, is_long)
            outs = []
            for h in range(heads):
                query = head_parts(proj, rows, h, 0) * head_masks[h % 2]
                scores = nt(query, head_parts(proj, rows, h, 1)) * 0.125
                scores = jnp.where(keep, scores, -1e30)
                weights = jnp.exp(scores - jnp.max(scores, axis=1, keepdims=True))
                weights = weights / jnp.sum(weights, axis=1, keepdims=True)
                probs[k, model, h] = weights
                outs.append(nn(weights.astype(bf16), head_parts(proj, rows, h, 2)))
            for g in range(pad // BLOCK):
                second = outs[2 * g + 1] if 2 * g + 1 < heads else jnp.zeros((BLOCK, BLOCK), f32)
                both = jnp.where(first_half, outs[2 * g], second)
                att[rows, pl.ds(g * BLOCK, BLOCK)] = both.astype(bf16)

        for is_long, low_model in ((True, 0), (False, long_blocks)):
            def one(at, carry, is_long=is_long, low_model=low_model):
                block(is_long, low_model + at)
                return carry

            lax.fori_loop(0, long_blocks, one, 0)

        def mix(at):
            rows = pl.ds(pl.multiple_of(k * span + at, 256), 256)
            s.partial[k, pl.ds(at, 256), :] = nn(att[rows, :], mixw[...])

        tiles(span, 256, mix)

    def pipeline(gathers, work, before=None, after=None, forwarded=None):
        scatters = []
        for k in range(chunks):
            if gathers:
                gathers[k].forward()
            if forwarded is not None:
                forwarded(k)
            if k:
                scatters[k - 1].middle()
            if gathers:
                gathers[k].finish()
            if before is not None:
                before(k)
            work(k)
            scatters.append(Scatter(k))
            if after is not None:
                after(k)
        scatters[-1].middle()
        return scatters

    scatters = pipeline(gathers, attend)

    gain_one, shift_one, gain_two, shift_two = [
        ref[...].reshape(1, width)
        for ref in (gain_one_ref, shift_one_ref, gain_two_ref, shift_two_ref)
    ]
    norm, act, slope = s.norm, s.act, s.slope
    gathers = []
    for k in range(chunks):
        hidden = x[rows_of(m, k), :].astype(f32) + scatters[k].end()
        normal, scale = norm_forward(hidden)
        s.normal_one[own_rows(k), :] = normal
        s.scale_one[own_rows(k), :] = jnp.broadcast_to(scale, (BLOCK, 128))
        normed = normal * gain_one + shift_one
        s.normed[own_rows(k), :] = normed
        norm[rows_of(m, k), :] = normed.astype(bf16)
        gathers.append(Gather(norm, k))

    def feed(k):
        def one(at):
            rows = pl.ds(pl.multiple_of(k * span + at, 128), 128)
            pre = nn(norm[rows, :], upw[...])
            cumulative = 0.5 * (1.0 + lax.erf(pre * 0.7071067811865476))
            act[rows, :] = (pre * cumulative).astype(bf16)
            slope[rows, :] = cumulative + pre * (0.3989422804014327 * jnp.exp(-0.5 * pre * pre))

        tiles(span, 128, one)

        def two(at):
            rows = pl.ds(pl.multiple_of(k * span + at, 256), 256)
            s.partial[k, pl.ds(at, 256), :] = nn(act[rows, :], downw[...])

        tiles(span, 256, two)

    scatters = pipeline(gathers, feed)

    for k in range(chunks):
        hidden = s.normed[own_rows(k), :] + scatters[k].end()
        normal, scale = norm_forward(hidden)
        s.normal_two[own_rows(k), :] = normal
        s.scale_two[own_rows(k), :] = jnp.broadcast_to(scale, (BLOCK, 128))
        rows_now = normal * gain_two + shift_two
        s.rows[own_rows(k), :] = rows_now
        block_out[own_rows(k), :] = rows_now.astype(bf16)

    gb, gp, gm, gproj = s.gb, s.gp, s.gm, s.gproj

    def second_back(k):
        rows = own_rows(k)
        return norm_back(
            s.grad_rows[rows, :], s.normal_two[rows, :], s.scale_two[rows, 0:1], gain_two
        )

    s.grad_rows[...] = s.upper[...].astype(f32)
    gathers = []
    for k in range(chunks):
        gb[rows_of(m, k), :] = second_back(k).astype(bf16)
        gathers.append(Gather(gb, k))

    pool = s.pool
    half = width // 2
    firsts = jnp.concatenate(
        [s.rows[pl.ds(i * SHORT_LEN, 1), :] for i in range(per_short)], axis=0
    )
    pool[d, m] = jnp.concatenate([firsts[:, :half], firsts[:, half:]], axis=0).astype(bf16)

    def pool_copy(j):
        return pltpu.make_async_remote_copy(
            src_ref=pool.at[d, m],
            dst_ref=pool.at[d, m],
            send_sem=s.pool_send.at[j],
            recv_sem=s.pool_recv.at[j],
            device_id=(lax.rem(d + j, n_data), m),
            device_id_type=MESH,
        )

    def pool_start(j, carry):
        pool_copy(j).start()
        return carry

    def pool_arrived(j, carry):
        pool_copy(j).wait_recv()
        return carry

    def pool_sent(j, carry):
        pool_copy(j).wait_send()
        return carry

    lax.fori_loop(1, n_data, pool_start, 0)
    lax.fori_loop(1, n_data, pool_arrived, 0)
    far = net.send(pool.at[:, m], pool.at[:, m], by_side)
    near = net.send(pool.at[:, m], pool.at[:, m], by_core)
    far.wait_recv()
    passed = net.send(pool.at[:, m2], pool.at[:, m2], by_core)
    near.wait_recv()
    passed.wait_recv()


    count = devices * per_short
    sentences = dims.longs + dims.shorts
    pairs2 = pairing_ref.shape[1]

    def sentence_of(index):
        place = lax.div(index, per_short)
        slot = lax.rem(index, per_short)
        model = lax.rem(place, n_model)
        data = lax.div(place, n_model)
        ratio = LONG_LEN // SHORT_LEN
        is_long = model < long_blocks
        valid = jnp.logical_or(jnp.logical_not(is_long), lax.rem(slot, ratio) == 0)
        number = jnp.where(
            is_long,
            model * per_long + lax.div(slot, ratio),
            dims.longs + (model - long_blocks) * per_short + slot,
        )
        return jnp.where(valid, data * sentences + number, -1)

    group_rows_first = n_model * per_short

    def unfold(at, carry):
        part = pool[at].astype(f32)
        here = pl.ds(pl.multiple_of(at * group_rows_first, 16), group_rows_first)
        s.left[here, :] = part[:, :per_short, :].reshape(group_rows_first, half).astype(bf16)
        s.right[here, :] = part[:, per_short:, :].reshape(group_rows_first, half).astype(bf16)
        return carry

    lax.fori_loop(0, n_data, unfold, 0)
    gram, known = s.gram, s.known
    pair_col = column_of(pairing_ref[...].astype(f32)).astype(i32)
    step = 256 if count <= 256 else 128

    def measure(number, carry):
        at = number * step
        block = pl.ds(pl.multiple_of(at, 128), step)
        gram[:, block] = nt(s.left[...], s.left[block, :]) + nt(
            s.right[...], s.right[block, :]
        )
        sent = sentence_of(iota((1, step), 1) + at)
        place = jnp.sum(
            jnp.where(pair_col == sent, iota((pairs2, step), 0), 0).astype(f32),
            axis=0,
            keepdims=True,
        )
        place = jnp.where(sent >= 0, place, -2.0)
        pair = jnp.floor(place * 0.5)
        eye = iota((step, step), 0) == iota((step, step), 1)
        square = jnp.sum(jnp.where(eye, gram[block, block], 0.0), axis=0, keepdims=True)
        known[0:1, block] = lax.rsqrt(square + 1e-06)
        known[1:2, block] = pair
        known[2:3, block] = jnp.where(sent >= 0, place - 2.0 * pair, 5.0)
        for i in range(3):
            s.known_col[block, i : i + 1] = column_of(known[i : i + 1, block])
        return carry

    lax.fori_loop(0, count // step, measure, 0)

    def logits_of(part, block, inv_col, pair_col, side_col):
        inv_row, pair_row, side_row = known[0:1, block], known[1:2, block], known[2:3, block]
        facing = side_col + side_row == 1.0
        same = (pair_col == pair_row) & facing
        cosine = part * inv_col * inv_row
        return 40.0 * (cosine - jnp.where(same, 0.3, 0.0)), facing, same

    def lose(number, loss):
        block = pl.ds(pl.multiple_of(number * step, 128), step)
        logits, facing, same = logits_of(
            gram[:, block],
            block,
            s.known_col[:, 0:1],
            s.known_col[:, 1:2],
            s.known_col[:, 2:3],
        )
        masked = jnp.where(facing, logits, -1e30)
        top = jnp.max(masked, axis=0, keepdims=True)
        total = jnp.sum(jnp.where(facing, jnp.exp(masked - top), 0.0), axis=0, keepdims=True)
        valid = known[1:2, block] >= 0.0
        log_total = jnp.where(valid, top + jnp.log(jnp.where(valid, total, 1.0)), 0.0)
        known[3:4, block] = log_total
        matched = jnp.sum(jnp.where(same, logits, 0.0), axis=0, keepdims=True)
        return loss + jnp.sum(log_total - matched, axis=1, keepdims=True)

    loss = lax.fori_loop(0, count // step, lose, jnp.zeros((1, 1), f32))
    loss_out[...] = jnp.broadcast_to(loss * (2.0 / pairs2), loss_out.shape)

    own_first = pl.ds(pl.multiple_of(me * per_short, 8), per_short)
    mine_mask = iota((per_short, count), 1) == iota((per_short, count), 0) + me * per_short

    def own_col(row):
        return jnp.sum(jnp.where(mine_mask, row, 0.0), axis=1, keepdims=True)

    inv_row, log_row = known[0:1, :], known[3:4, :]
    inv_own, log_own = own_col(inv_row), own_col(log_row)
    logits, facing, same = logits_of(
        gram[own_first, :],
        slice(None),
        inv_own,
        own_col(known[1:2, :]),
        own_col(known[2:3, :]),
    )
    pull = jnp.exp(jnp.where(facing, logits - log_own, -1e30)) + jnp.exp(
        jnp.where(facing, logits - log_row, -1e30)
    )
    pull = 40.0 * (pull - jnp.where(same, 2.0, 0.0)) * inv_row
    pull_high = pull.astype(bf16)
    pull_low = (pull - pull_high.astype(f32)).astype(bf16)
    grad_unit = jnp.concatenate(
        [nn(pull_high, n[...]) + nn(pull_low, n[...]) for n in (s.left, s.right)], axis=1
    )
    unit = firsts * inv_own
    grad_firsts = inv_own * (
        grad_unit - unit * jnp.sum(unit * grad_unit, axis=1, keepdims=True)
    )
    grad_rows = s.grad_rows
    for i in range(per_short):
        at = pl.ds(i * SHORT_LEN, 1)
        grad_rows[at, :] = grad_rows[at, :] + grad_firsts[i : i + 1, :]


    norm_sum = s.norm_sum
    norm_sum[0] = jnp.zeros((8, width), f32)
    for k in range(chunks):
        s.second[own_rows(k), :] = second_back(k)
    patch = s.patch
    firsts = jnp.concatenate(
        [s.second[pl.ds(i * SHORT_LEN, 1), :] for i in range(per_short)], axis=0
    )
    patch[m] = jnp.concatenate([firsts[:, :half], firsts[:, half:]], axis=0).astype(bf16)
    far = net.send(patch.at[m], patch.at[m], by_side)
    near = net.send(patch.at[m], patch.at[m], by_core)
    for k in range(chunks):
        grad = grad_rows[own_rows(k), :]
        normal = s.normal_two[own_rows(k), :]
        norm_sum[0, 2:3, :] = norm_sum[0, 2:3, :] + jnp.sum(grad * normal, axis=0, keepdims=True)
        norm_sum[0, 3:4, :] = norm_sum[0, 3:4, :] + jnp.sum(grad, axis=0, keepdims=True)
    for k in range(chunks):
        gathers[k].forward()
    far.wait_recv()
    passed = net.send(patch.at[m2], patch.at[m2], by_core)
    for k in range(chunks):
        gathers[k].finish()
        net.sent(gathers[k].far)
        net.sent(gathers[k].near)
        net.sent(gathers[k].passed)
    near.wait_recv()
    passed.wait_recv()
    top_row = iota((16, width), 0) == 0
    per_chunk = BLOCK // SHORT_LEN

    def mend(model, carry):
        fresh = patch[model].astype(f32)
        for i in range(per_short):
            at = (i // per_chunk) * span + model * BLOCK + (i % per_chunk) * SHORT_LEN
            rows = pl.ds(pl.multiple_of(at, 16), 16)
            new = jnp.concatenate(
                [fresh[i : i + 1], fresh[per_short + i : per_short + i + 1]], axis=1
            )
            gb[rows, :] = jnp.where(top_row, new, gb[rows, :].astype(f32)).astype(bf16)
        return carry

    lax.fori_loop(0, n_model, mend, 0)

    def feed_back(k):
        def one(at):
            rows = pl.ds(pl.multiple_of(k * span + at, 128), 128)
            gp[rows, :] = (nt(gb[rows, :], downw[...]) * slope[rows, :]).astype(bf16)

        tiles(span, 128, one)

        def two(at):
            rows = pl.ds(pl.multiple_of(k * span + at, 256), 256)
            s.partial[k, pl.ds(at, 256), :] = nt(gp[rows, :], upw[...])

        tiles(span, 256, two)

    def weight_grad(target, base, rows, left, right, left_at=0):
        step = 64

        def one(at):
            part = tn(left[:, pl.ds(pl.multiple_of(left_at + at, 64), step)], right[...])
            target[pl.ds(pl.multiple_of(base + at, 16), step), :] = part.astype(bf16)

        tiles(rows, step, one)

    def whole_grad(target, base, left, right, keep=None):
        total = left.shape[1]
        for at in range(0, total, 256):
            part = tn(left[:, at : at + 256], right[...]).astype(bf16)
            size = 256 if keep is None else keep
            target[pl.ds(base + (at // 256) * size, size), :] = part[:size]

    bits = tuple(range(n_data.bit_length() - 1))
    half_rows = width // 2
    reduces = [
        Reduce(
            net,
            s.grads.at[pl.ds(i * half_rows, half_rows)],
            s.sums.at[pl.ds(i * half_rows, half_rows)],
            s.sum_land.at[i],
            (d, m),
            bits,
        )
        for i in range(6)
    ]
    downs, ups, heads_sums = reduces[0:2], reduces[2:4], reduces[4:6]

    def steps(*order):
        for at in order:
            reduces[at].step()

    def begin(items, base, left, right):
        for i, item in enumerate(items):
            for at in range(i * half_rows, (i + 1) * half_rows, half_rows):
                part = tn(left[:, at : at + half_rows], right[...])
                s.grads[pl.ds(base + at, half_rows), :] = part.astype(bf16)
            item.start()

    begin(downs, 0, act, gb)
    scatters = pipeline([], feed_back)
    begin(ups, width, norm, gp)
    gathers = []
    for k in range(chunks):
        grad = s.second[own_rows(k), :] + scatters[k].end()
        normal = s.normal_one[own_rows(k), :]
        norm_sum[0, 0:1, :] = norm_sum[0, 0:1, :] + jnp.sum(grad * normal, axis=0, keepdims=True)
        norm_sum[0, 1:2, :] = norm_sum[0, 1:2, :] + jnp.sum(grad, axis=0, keepdims=True)
        back = norm_back(grad, normal, s.scale_one[own_rows(k), 0:1], gain_one)
        s.second[own_rows(k), :] = back
        gm[rows_of(m, k), :] = back.astype(bf16)
        gathers.append(Gather(gm, k))
        steps(0)

    def attend_back(k):
        def unmix(at):
            rows = pl.ds(pl.multiple_of(k * span + at, 256), 256)
            s.gatt[rows, :] = nt(gm[rows, :], mixw[...]).astype(bf16)

        tiles(span, 256, unmix)

        def block(model, carry):
            rows = rows_of(model, k)
            parts = ([], [], [])
            for h in range(heads):
                g = h // 2
                mask = head_masks[h % 2]
                grad_out = s.gatt[rows, pl.ds(g * BLOCK, BLOCK)] * mask
                weights = probs[k, model, h]
                grad_probs = nt(grad_out, head_parts(proj, rows, h, 2))
                inner = jnp.sum(weights * grad_probs, axis=1, keepdims=True)
                grad_scores = (weights * (grad_probs - inner)).astype(bf16)
                parts[0].append(nn(grad_scores, head_parts(proj, rows, h, 1)) * 0.125)
                parts[1].append(tn(grad_scores, head_parts(proj, rows, h, 0)) * 0.125)
                parts[2].append(tn(weights.astype(bf16), grad_out))
            for part in range(3):
                for g in range(pad // BLOCK):
                    outs = parts[part]
                    zero = jnp.zeros((BLOCK, BLOCK), f32)
                    second = outs[2 * g + 1] if 2 * g + 1 < heads else zero
                    both = jnp.where(first_half, outs[2 * g], second)
                    gproj[rows, pl.ds(part * pad + g * BLOCK, BLOCK)] = both.astype(bf16)
            return carry

        lax.fori_loop(0, n_model, block, 0)

        def one(at):
            rows = pl.ds(pl.multiple_of(k * span + at, 256), 256)
            s.partial[k, pl.ds(at, 256), :] = nn(gproj[rows, :], wt[...])

        tiles(span, 256, one)

    def forwarded(k):
        if k == 0:
            steps(1)

    def before_attend(k):
        if k == chunks - 1:
            steps(2)

    def after_attend(k):
        if k == 0:
            steps(0, 1)

    scatters = pipeline(gathers, attend_back, before_attend, after_attend, forwarded)
    steps(0, 1, 2)
    whole_grad(s.grads, 2 * width, att, gm, cols)
    whole_grad(s.grads, 2 * width + cols, gproj, x, cols)
    for item in heads_sums:
        item.start()
    steps(3, 0, 2, 1)
    swap_sent(s.returned, row_sems)
    for k in range(chunks):
        grad = s.second[own_rows(k), :] + scatters[k].end()
        s.grad_in[own_rows(k), :] = grad.astype(bf16)

    def pack(at):
        rows = pl.ds(at, 256)
        s.outgoing[rows, :] = nn(s.place[rows, :], s.grad_in[...]).astype(bf16)

    tiles(slots, 256, pack)
    swap_start(s.outgoing, s.incoming, out_sems)

    stages = [by_core, by_side]
    for bit in bits:
        stages.append(reduces[0].partner(bit)[1])

    def norm_step(at):
        copy = net.send(norm_sum.at[at], s.norm_land.at[at], stages[at])
        copy.wait_recv()
        norm_sum[at + 1] = norm_sum[at] + s.norm_land[at]

    order = [3, 1, 2, 3, 4, 2, 4, 5, 3, 4, 5, 3, 0, 1, 4, 5, 2, 4, 5, 3, 5, 4, 5]
    turn = 0
    while turn < len(stages) or any(item.todo for item in reduces):
        if turn < len(stages):
            norm_step(turn)
        if not order:
            order = [i for i, item in enumerate(reduces) if item.todo]
        for at in order[:4]:
            if reduces[at].todo:
                steps(at)
        order = order[4:]
        turn += 1
    norm_out[...] = norm_sum[len(stages)]
    swap_arrived(s.incoming, out_sems)
    outs = [
        pltpu.make_async_copy(s.sums, weight_out, s.load_sems.at[0]),
        pltpu.make_async_copy(s.incoming, incoming_out, s.load_sems.at[1]),
    ]
    for copy in outs:
        copy.start()
    for copy in outs:
        copy.wait()
    net.drain()
    lax.fori_loop(1, n_data, pool_sent, 0)
    swap_sent(s.asked, ask_sems)
    swap_sent(s.incoming, out_sems)


def table_kernel(
    cols,
    ids_ref,
    norm_ref,
    loss_ref,
    incoming_hbm,
    weights_hbm,
    table_hbm,
    first_hbm,
    second_hbm,
    step_hbm,
    first_out,
    second_out,
    down_out,
    up_out,
    mix_out,
    heads_out,
    loss_out,
    *rest,
):
    norm_outs = rest[:4]
    incoming, low, wide, state, in_sems, out_sems, low_sems, wide_sems = rest[4:]
    slots, width = incoming.shape
    parts = in_sems.shape[1]
    rows = state.shape[1] // parts

    def tile(at):
        return pl.ds(pl.multiple_of(at * rows, 8), rows)

    def load(i, at):
        src = (first_hbm, second_hbm, table_hbm)[i]
        return pltpu.make_async_copy(
            src.at[tile(at)], state.at[i, tile(at)], in_sems.at[i, at]
        )

    def store(i, at):
        dst = (first_out, second_out, step_hbm)[i]
        return pltpu.make_async_copy(
            state.at[i, tile(at)], dst.at[tile(at)], out_sems.at[i, at]
        )

    def each_part(step):
        def one(at, carry):
            for i in range(3):
                step(i, at)
            return carry

        lax.fori_loop(0, parts, one, 0)

    named = pltpu.make_async_copy(incoming_hbm, incoming, low_sems.at[0])
    named.start()
    lows = []
    for i in range(3):
        here = pl.ds(i * width, width)
        lows.append(
            pltpu.make_async_copy(weights_hbm.at[here], low.at[here], low_sems.at[1 + i])
        )
    for copy in lows[:1]:
        copy.start()
    each_part(lambda i, at: load(i, at).start())
    for copy in lows[1:]:
        copy.start()
    loss_out[...] = loss_ref[0:1, 0:1]
    for i, out in enumerate(norm_outs):
        out[...] = norm_ref[i, :]
    named.wait()

    wides = []
    starts = (0, width, 2 * width, 2 * width + cols, 3 * width)
    for i, out in enumerate((down_out, up_out, mix_out, heads_out)):
        here = pl.ds(starts[i], starts[i + 1] - starts[i])
        wides.append(pltpu.make_async_copy(wide.at[here], out, wide_sems.at[i]))

    def widen(i):
        lows[i].wait()
        step = 96

        def one(at, carry):
            here = pl.ds(pl.multiple_of(i * width + at * step, 16), step)
            wide[here, :] = low[here, :].astype(f32)
            return carry

        lax.fori_loop(0, width // step, one, 0)
        for copy in wides[i : i + 1] if i < 2 else wides[2:]:
            copy.start()

    widen(0)

    def update(at, carry):
        for i in range(3):
            load(i, at).wait()
        here = tile(at)
        hot = (iota((rows, slots), 0) + at * rows == ids_ref[0:1, :]).astype(f32)
        uses = jnp.sum(hot, axis=1, keepdims=True)
        row_grad = nn(hot.astype(bf16), incoming[...]) * (1.0 / jnp.maximum(uses, 1.0))
        first_new = 0.9 * state[0, here, :] + 0.1 * row_grad
        second_new = 0.95 * state[1, here, :] + 0.05 * row_grad * row_grad
        state[0, here, :] = first_new
        state[1, here, :] = second_new
        scale = jnp.sqrt(second_new * (1.0 / second_fix)) + 1e-08
        state[2, here, :] = first_new * (1.0 / first_fix) / scale + 0.01 * state[2, here, :]
        for i in range(3):
            store(i, at).start()
        return carry

    lax.fori_loop(0, parts, update, 0)
    widen(1)
    widen(2)
    each_part(lambda i, at: store(i, at).wait())
    for copy in wides:
        copy.wait()


def body(
    token_owner,
    token_row,
    long_len,
    short_len,
    pairing,
    embed_table,
    first_moment,
    second_moment,
    heads_weight,
    mix_weight,
    up_weight,
    down_weight,
    first_gain,
    first_shift,
    second_gain,
    second_shift,
    upper_grad,
):
    tok, width = upper_grad.shape
    n_model, n_data = lax.axis_size("mp"), lax.axis_size("dp")
    devices = n_model * n_data
    group = tok * n_model
    cols = heads_weight.shape[2]
    pad = -(-cols // BLOCK) * BLOCK
    ff = up_weight.shape[1]
    slots = devices * SLOTS
    chunks = tok // BLOCK
    span = BLOCK * n_model
    per_short = tok // SHORT_LEN
    firsts = devices * per_short
    table_rows = embed_table.shape[0]
    bits = n_data.bit_length() - 1
    n_sems = 96 + 16 * bits
    vmem = pltpu.VMEM
    dma = pltpu.SemaphoreType.DMA
    shapes = dict(
        stage=vmem((chunks, span, width), f32),
        table=vmem((table_rows, width), bf16),
        wt=vmem((3 * pad, width), bf16),
        mixw=vmem((pad, width), bf16),
        upw=vmem((width, ff), bf16),
        downw=vmem((ff, width), bf16),
        upper=vmem((tok, width), bf16),
        ask=vmem((slots, 128), bf16),
        asked=vmem((slots, 128), bf16),
        place=vmem((slots, tok), bf16),
        pick=vmem((tok, slots), bf16),
        found=vmem((slots, width), bf16),
        returned=vmem((slots, width), bf16),
        x=vmem((group, width), bf16),
        proj=vmem((group, 3 * pad), bf16),
        att=vmem((group, pad), bf16),
        gatt=vmem((group, pad), bf16),
        probs=vmem((chunks, n_model, cols // HEAD, BLOCK, BLOCK), f32),
        near_send=vmem((chunks, 2, BLOCK, width), bf16),
        near_land=vmem((chunks, 2, BLOCK, width), bf16),
        far_send=vmem((chunks, BLOCK, width), bf16),
        far_land=vmem((chunks, BLOCK, width), bf16),
        normal_one=vmem((tok, width), f32),
        scale_one=vmem((tok, 128), f32),
        normed=vmem((tok, width), f32),
        norm=vmem((group, width), bf16),
        act=vmem((group, ff), bf16),
        slope=vmem((group, ff), f32),
        normal_two=vmem((tok, width), f32),
        scale_two=vmem((tok, 128), f32),
        rows=vmem((tok, width), f32),
        grad_rows=vmem((tok, width), f32),
        patch=vmem((n_model, 2 * per_short, width // 2), bf16),
        pool=vmem((n_data, n_model, 2 * per_short, width // 2), bf16),
        left=vmem((firsts, width // 2), bf16),
        right=vmem((firsts, width // 2), bf16),
        gram=vmem((firsts, firsts), f32),
        known=vmem((8, firsts), f32),
        known_col=vmem((firsts, 128), f32),
        gb=vmem((group, width), bf16),
        gm=vmem((group, width), bf16),
        second=vmem((tok, width), f32),
        grad_in=vmem((tok, width), bf16),
        norm_sum=vmem((3 + bits, 8, width), f32),
        norm_land=vmem((2 + bits, 8, width), f32),
        grads=vmem((3 * width, width), bf16),
        sums=vmem((3 * width, width), bf16),
        sum_land=vmem((6, width, width // 2), bf16),
        send_sems=dma((n_sems,)),
        recv_sems=dma((n_sems,)),
        load_sems=dma((16,)),
        ask_send=dma((devices,)),
        ask_recv=dma((devices,)),
        row_send=dma((devices,)),
        row_recv=dma((devices,)),
        out_send=dma((devices,)),
        out_recv=dma((devices,)),
        pool_send=dma((n_data,)),
        pool_recv=dma((n_data,)),
    )
    dims = SimpleNamespace(
        n_data=n_data,
        n_model=n_model,
        names=tuple(shapes),
        tok=tok,
        width=width,
        cols=cols,
        pad=pad,
        ff=ff,
        longs=long_len.shape[1],
        shorts=short_len.shape[1],
    )
    in_vmem = pl.BlockSpec(memory_space=pltpu.VMEM)
    in_smem = pl.BlockSpec(memory_space=pltpu.SMEM)
    in_hbm = pl.BlockSpec(memory_space=pl.ANY)
    heads_rows = jnp.transpose(heads_weight, (1, 2, 0)).reshape(3 * cols, width)
    block_out, weights, norms, loss, incoming, ids = pl.pallas_call(
        functools.partial(layer_kernel, dims),
        out_shape=(
            jax.ShapeDtypeStruct((tok, width), bf16),
            jax.ShapeDtypeStruct((3 * width, width), bf16),
            jax.ShapeDtypeStruct((8, width), f32),
            jax.ShapeDtypeStruct((8, 128), f32),
            jax.ShapeDtypeStruct((slots, width), bf16),
            jax.ShapeDtypeStruct((8, slots), i32),
        ),
        in_specs=[in_vmem, in_vmem, in_smem, in_smem] + [in_vmem] * 5 + [in_hbm] * 6,
        out_specs=(in_vmem, in_hbm, in_vmem, in_vmem, in_hbm, in_vmem),
        scratch_shapes=list(shapes.values()),
        compiler_params=pltpu.CompilerParams(
            collective_id=0, has_side_effects=True, vmem_limit_bytes=63 * 2**20
        ),
    )(
        token_owner.reshape(1, group),
        token_row.reshape(1, group),
        long_len,
        short_len,
        pairing.reshape(1, -1),
        first_gain,
        first_shift,
        second_gain,
        second_shift,
        embed_table,
        heads_rows,
        mix_weight,
        up_weight,
        down_weight,
        upper_grad,
    )
    parts = 8
    whole = jax.ShapeDtypeStruct((table_rows, width), f32)
    table_step, first_new, second_new, down_grad, up_grad, mix_grad, heads_grad, loss, *norm_grads = (
        pl.pallas_call(
            functools.partial(table_kernel, cols),
            out_shape=(whole, whole, whole)
            + tuple(
                jax.ShapeDtypeStruct((rows, width), f32) for rows in (ff, width, cols, 3 * cols)
            )
            + (jax.ShapeDtypeStruct((1, 1), f32),)
            + (jax.ShapeDtypeStruct((width,), f32),) * 4,
            in_specs=[in_vmem] * 3 + [in_hbm] * 5,
            out_specs=(in_hbm,) * 7 + (in_vmem,) * 5,
            scratch_shapes=[
                vmem((slots, width), bf16),
                vmem((3 * width, width), bf16),
                vmem((3 * width, width), f32),
                vmem((3, table_rows, width), f32),
                dma((3, parts)),
                dma((3, parts)),
                dma((4,)),
                dma((4,)),
            ],
            compiler_params=pltpu.CompilerParams(vmem_limit_bytes=63 * 2**20),
        )(ids, norms, loss, incoming, weights, embed_table, first_moment, second_moment)
    )
    return (
        loss.reshape(()),
        block_out,
        jnp.transpose(heads_grad.reshape(3, cols, width), (2, 0, 1)),
        mix_grad,
        up_grad,
        down_grad,
        *norm_grads,
        table_step,
        first_new,
        second_new,
    )


def solution(mesh):
    rows = P(("dp", "mp"), None)
    in_specs = (
        P("dp", None),
        P("dp"),
        P("dp", None),
        P("dp", None),
        P(),
        rows,
        rows,
        rows,
        P(None, None, "mp"),
        P("mp", None),
        P(None, "mp"),
        P("mp", None),
        P(),
        P(),
        P(),
        P(),
        rows,
    )
    out_specs = (
        P(),
        rows,
        P(None, None, "mp"),
        P("mp", None),
        P(None, "mp"),
        P("mp", None),
        P(),
        P(),
        P(),
        P(),
        rows,
        rows,
        rows,
    )
    return jax.shard_map(body, mesh=mesh, in_specs=in_specs, out_specs=out_specs, check_vma=False)
```

time: 794 us -> 240 us (0.30)
  waiting for transfers between devices: 337 us -> 0 us
  Pallas kernels: 0 us -> 238 us
  blocking collectives: 192 us -> 0 us
  other arithmetic: 111 us -> 0 us
  local copies, waits for them, and re-layouts: 64.9 us -> 0.75 us
  matrix products: 55.6 us -> 0 us
  between operations: 17.6 us -> 0.68 us
  starting transfers between devices: 9.01 us -> 0 us
    pallas_call x0 -> x2, Pallas kernels: none -> 238 us  [the longest x1 220 us: body(): pl.pallas_call(functools.partial(layer_kernel, dims), out_shape=(jax.Shap...]
    psum x1 -> x0, blocking collectives: 135 us -> none  [body(): lax.psum((grad_gain_one, grad_shift_one, grad_gain_two, grad_shift_two),...]
    reduce_scatter x3 -> x0, waiting for transfers between devices: 109 us -> none  [the longest x1 38.1 us: body(): lax.psum_scatter(jnp.dot(grad_pre, up_weight.T, preferred_element_type=jn...]
    psum x1 -> x0, waiting for transfers between devices: 107 us -> none  [body(): lax.psum((grad_heads, grad_mix, grad_up, grad_down), 'dp')]
    all_to_all x2 -> x0, waiting for transfers between devices: 71.1 us -> none  [the longest x1 71.1 us: body(): lax.all_to_all(looked, ('dp', 'mp'), split_axis=0, concat_axis=0, tiled=T...]
    dot_general x21 -> x0, matrix products: 55.6 us -> none  [the longest x4 13.2 us: rows_product(): lax.dot_general(left, right, (((0,), (0,)), ((), ())), preferred_element_...]
    all_gather x3 -> x0, waiting for transfers between devices: 49.8 us -> none  [the longest x1 19.6 us: body(): ffn_in = lax.all_gather(normed_low, 'mp', axis=0, tiled=True)]
    scatter-add x7 -> x0, other arithmetic: 44.7 us -> none  [the longest x1 17.7 us: body(): row_sum = jnp.zeros((table_rows, width), jnp.float32).at[flat_rows].add(i...]
  transfers between devices with their start and end apart: 9 -> 0, of which waited for: 8 -> 0; matrix products, arithmetic and copies ran while one was open for 8% -> 0% of each run, Pallas kernels for 0% -> 0%
where the time goes in v1:
time: 240 us; the launch traced here: 239 us
  Pallas kernels  238 us (99%)
    pallas_call x1, Pallas kernels, body(): pl.pallas_call(functools.partial(layer_kernel, dims), out_shape=(jax.Shap...  220 us
    pallas_call x1, Pallas kernels, body(): pl.pallas_call(functools.partial(table_kernel, cols), out_shape=(whole, w...  18.5 us

profile of v1, /device:TPU:0, one launch (start us, length us, event | category | flops | bytes accessed | tf_op | source)
XLA Modules:
  0.0 239.5 jit_solution(5071588478424541804)
XLA Ops:
  0.7 219.6 %shard_map.264 = (bf16[256,768]{1,0:T(8,128)(2,1)}, bf16[2304,768]{1,0:T(8,128)(2,1)}, f32[8,768]{1,0:T(8,128)}, f32[8,128]{1,0:T(8,128)}, bf16[512,768]{1,0:T(8,128)(2,1)}, /*index=5*/s32[8,512]{1,0:T(8,128)}) custom-call(s32[1,1024]{1,0:T(1,128)} %bitcast.11, s32[1,1024]{1,0:T(1,128)} %bitcast.12, s32[1,4]{1,0:T(1,128)} %long_ref.1, s32[1,16]{1,0:T(1,128)} %short_ref.1, ...), custom_call_target="tpu_custom_call" | custom-call | tf_op jit(solution)/shard_map/pallas_call | solution.py:1210
  220.3 0.0 copy-start
  220.3 18.5 %shard_map.265 = (f32[2048,768]{1,0:T(8,128)}, f32[2048,768]{1,0:T(8,128)}, f32[2048,768]{1,0:T(8,128)}, f32[768,768]{1,0:T(8,128)}, f32[768,768]{1,0:T(8,128)},...) custom-call(s32[8,512]{1,0:T(8,128)} %get-tuple-element.31.ids_ref, ...), custom_call_target="tpu_custom_call" | custom-call | tf_op jit(solution)/shard_map/pallas_call | solution.py:1246
  238.7 0.0 copy-done
  238.7 0.7 copy.31
Async XLA Ops:
  220.3 18.5 %copy-start = (bf16[256,768]{1,0:T(8,128)(2,1)S(1)}, bf16[256,768]{1,0:T(8,128)(2,1)}, u32[]{:S(2)}) copy-start(bf16[256,768]{1,0:T(8,128)(2,1)} %get-tuple-element.63) | copy-start | bytes 1179652

commit v2 on v1

--- a/solution.py
+++ b/solution.py
@@ -13,6 +13,7 @@
 SHORT_LEN = 32
 BLOCK = 128
 SLOTS = 16
+NORM = -1
 MESH = pl.DeviceIdType.MESH
 bf16 = jnp.bfloat16
 f32 = jnp.float32
@@ -62,32 +63,39 @@
 class Net:
     def __init__(self, send_sems, recv_sems):
         self.send_sems, self.recv_sems = send_sems, recv_sems
+        self.open = [None] * send_sems.shape[0]
         self.count = 0
-        self.open = []
-
-    def send(self, src, dst, device):
-        at = self.count
+        self.names = {}
+
+    def send(self, src, dst, device, name=None):
+        slot = self.count % len(self.open)
+        if self.open[slot] is not None:
+            self.open[slot].wait_send()
+        at = self.names.setdefault(self.count if name is None else name, len(self.names))
         self.count += 1
         copy = pltpu.make_async_remote_copy(
             src_ref=src,
             dst_ref=dst,
-            send_sem=self.send_sems.at[at],
+            send_sem=self.send_sems.at[slot],
             recv_sem=self.recv_sems.at[at],
             device_id=device,
             device_id_type=MESH,
         )
         copy.start()
-        self.open.append(copy)
+        self.open[slot] = copy
         return copy
 
     def sent(self, copy):
-        copy.wait_send()
-        self.open = [item for item in self.open if item is not copy]
+        for slot, item in enumerate(self.open):
+            if item is copy:
+                copy.wait_send()
+                self.open[slot] = None
 
     def drain(self):
         for copy in self.open:
-            copy.wait_send()
-        self.open = []
+            if copy is not None:
+                copy.wait_send()
+        self.open = [None] * len(self.open)
 
 
 class Reduce:
@@ -105,7 +113,8 @@
         self.todo = [self.add] * len(bits) + [self.grow] * grows
 
     def step(self):
-        self.todo.pop(0)()
+        if self.todo:
+            self.todo.pop(0)()
 
     def halves(self, stage):
         return stage == 0 or (self.part.shape[0] >> (stage - 1)) % 32 == 0
@@ -142,7 +151,7 @@
             self.net.sent(self.copy)
         target = self.whole if last else self.part
         cols = pl.ds(self.col, self.half)
-        step = 48
+        step = 48 if self.len % 48 == 0 else min(self.len, 64)
         now, row, part = self.now, self.row, self.part
 
         def tile(at, carry):
@@ -180,37 +189,35 @@
 
 def layer_kernel(
     dims,
-    owner_ref,
-    rowid_ref,
-    long_ref,
-    short_ref,
-    pairing_ref,
-    gain_one_ref,
-    shift_one_ref,
-    gain_two_ref,
-    shift_two_ref,
+    owner_hbm,
+    rowid_hbm,
+    long_hbm,
+    short_hbm,
+    pairing_hbm,
+    gain_one_hbm,
+    shift_one_hbm,
+    gain_two_hbm,
+    shift_two_hbm,
     table_hbm,
     heads_hbm,
     mix_hbm,
     up_hbm,
     down_hbm,
     upper_hbm,
+    first_hbm,
+    second_hbm,
     block_out,
-    weight_out,
     norm_out,
     loss_out,
-    incoming_out,
-    ids_out,
-    *scratch,
+    *rest,
 ):
+    resident = dims.resident
+    if resident:
+        sums, step_out, first_out, second_out, *scratch = rest
+    else:
+        weight_out, incoming_out, ids_hbm, *scratch = rest
     n_data, n_model = dims.n_data, dims.n_model
     s = SimpleNamespace(**dict(zip(dims.names, scratch, strict=True)))
-    group_rows = dims.tok * n_model
-    s.partial = s.stage
-    s.gproj = s.table.at[pl.ds(0, group_rows)]
-    s.gp = s.table.at[pl.ds(group_rows, group_rows)]
-    s.outgoing = s.found
-    s.incoming = s.returned
     tok, width, cols, pad, ff = dims.tok, dims.width, dims.cols, dims.pad, dims.ff
     devices = n_data * n_model
     group = tok * n_model
@@ -218,6 +225,20 @@
     span = BLOCK * n_model
     slots = devices * SLOTS
     table_rows = table_hbm.shape[0]
+
+    if resident:
+        wide_a, wide_b = first_out, second_out
+    else:
+        wide_a, wide_b, sums = s.wide_a, s.wide_b, s.sums
+    slope = wide_a.at[pl.ds(0, group)]
+    partial = [wide_a.at[pl.ds(group + k * span, span)] for k in range(chunks)]
+    s.normal_one, s.normed, s.normal_two, s.rows, s.grad_rows, s.second = [
+        wide_b.at[pl.ds(i * tok, tok)] for i in range(6)
+    ]
+    s.gproj = s.table.at[pl.ds(0, group)]
+    s.gp = s.table.at[pl.ds(group, group)]
+    s.outgoing = s.found
+    s.incoming = s.returned
     d = lax.axis_index("dp")
     m = lax.axis_index("mp")
     me = d * n_model + m
@@ -236,6 +257,27 @@
     def other(j):
         return lax.rem(me + j, devices)
 
+    owner_ref, rowid_ref, long_ref, short_ref = s.owner, s.rowid, s.long, s.short
+    pairing_ref = s.pairing
+    small = [
+        pltpu.make_async_copy(src, dst, s.small_sems.at[i])
+        for i, (src, dst) in enumerate(
+            (
+                (owner_hbm, s.owner),
+                (rowid_hbm, s.rowid),
+                (long_hbm, s.long),
+                (short_hbm, s.short),
+                (pairing_hbm, s.pairing),
+                (gain_one_hbm, s.gain_one),
+                (shift_one_hbm, s.shift_one),
+                (gain_two_hbm, s.gain_two),
+                (shift_two_hbm, s.shift_two),
+            )
+        )
+    ]
+    for copy in small:
+        copy.start()
+
     barrier = pltpu.get_barrier_semaphore()
 
     def greet(j, carry):
@@ -244,22 +286,28 @@
 
     lax.fori_loop(1, devices, greet, 0)
 
-    stage_rows = s.stage.shape[1]
+    stage_rows = table_rows // 4 if resident else span
     table_parts = table_rows // stage_rows
+
+    def table_part(at):
+        if resident:
+            return step_out.at[pl.ds(at * stage_rows, stage_rows)]
+        return partial[at % 2]
 
     def table_copy(at):
         return pltpu.make_async_copy(
             table_hbm.at[pl.ds(at * stage_rows, stage_rows)],
-            s.stage.at[at % 2],
-            s.load_sems.at[at % 2],
-        )
-
-    table_copy(0).start()
-    table_copy(1).start()
+            table_part(at),
+            s.table_sems.at[at],
+        )
+
+    ahead = table_parts if resident else 2
+    for at in range(ahead):
+        table_copy(at).start()
     loads = []
 
     def load(src, dst):
-        copy = pltpu.make_async_copy(src, dst, s.load_sems.at[2 + len(loads)])
+        copy = pltpu.make_async_copy(src, dst, s.load_sems.at[len(loads)])
         copy.start()
         loads.append(copy)
 
@@ -273,6 +321,8 @@
     load(down_hbm, downw)
     load(upper_hbm, s.upper)
 
+    for copy in small:
+        copy.wait()
     own_at = pl.multiple_of(m * tok, 128)
     owner_row = owner_ref[:, pl.ds(own_at, tok)]
     rowid_row = rowid_ref[:, pl.ds(own_at, tok)]
@@ -305,24 +355,12 @@
         return pl.ds(pl.multiple_of(place * SLOTS, SLOTS), SLOTS)
 
     def swap_copy(src, dst, sems, to):
-        send_sems, recv_sems = sems
         return pltpu.make_async_remote_copy(
             src_ref=src.at[slot_rows(to)],
             dst_ref=dst.at[slot_rows(me)],
-            send_sem=send_sems.at[to],
-            recv_sem=recv_sems.at[me],
+            send_sem=sems.at[0],
+            recv_sem=sems.at[1],
             device_id=at_device(to),
-            device_id_type=MESH,
-        )
-
-    def arrival(dst, sems, place):
-        send_sems, recv_sems = sems
-        return pltpu.make_async_remote_copy(
-            src_ref=dst.at[slot_rows(place)],
-            dst_ref=dst.at[slot_rows(place)],
-            send_sem=send_sems.at[place],
-            recv_sem=recv_sems.at[place],
-            device_id=at_device(place),
             device_id_type=MESH,
         )
 
@@ -334,29 +372,23 @@
         lax.fori_loop(1, devices, one, 0)
         dst[slot_rows(me), :] = src[slot_rows(me), :]
 
+    def swap_wait(dst, sem):
+        blocks = dst.at[pl.ds(0, slots - SLOTS)]
+        pltpu.make_async_copy(blocks, blocks, sem).wait()
+
     def swap_arrived(dst, sems):
-        def one(j, carry):
-            arrival(dst, sems, other(j)).wait_recv()
-            return carry
-
-        lax.fori_loop(1, devices, one, 0)
+        swap_wait(dst, sems.at[1])
 
     def swap_sent(dst, sems):
-        def one(j, carry):
-            arrival(dst, sems, other(j)).wait_send()
-            return carry
-
-        lax.fori_loop(1, devices, one, 0)
-
-    ask_sems = (s.ask_send, s.ask_recv)
-    row_sems = (s.row_send, s.row_recv)
-    out_sems = (s.out_send, s.out_recv)
+        swap_wait(dst, sems.at[0])
+
+    ask_sems, row_sems, out_sems = s.ask_sems, s.row_sems, s.out_sems
     swap_start(s.ask, s.asked, ask_sems)
     for at in range(table_parts):
         table_copy(at).wait()
-        s.table[pl.ds(at * stage_rows, stage_rows), :] = s.stage[at % 2].astype(bf16)
-        if at + 2 < table_parts:
-            table_copy(at + 2).start()
+        s.table[pl.ds(at * stage_rows, stage_rows), :] = table_part(at)[...].astype(bf16)
+        if at + ahead < table_parts:
+            table_copy(at + ahead).start()
     swap_arrived(s.asked, ask_sems)
 
     per_block = BLOCK // SLOTS
@@ -368,7 +400,7 @@
         ident = asked[:, 0:1] * 64.0 + asked[:, 64:65] - 1.0
         eye = iota((BLOCK, BLOCK), 0) == iota((BLOCK, BLOCK), 1)
         ident_row = jnp.sum(jnp.where(eye, ident, 0.0), axis=0, keepdims=True)
-        ids_out[:, rows] = jnp.broadcast_to(ident_row.astype(i32), (8, BLOCK))
+        s.ids[:, rows] = jnp.broadcast_to(ident_row.astype(i32), (8, BLOCK))
         hot = (iota((BLOCK, table_rows), 1) == ident.astype(i32)).astype(f32).astype(bf16)
         s.found[rows, :] = nn(hot, s.table[...]).astype(bf16)
 
@@ -400,13 +432,13 @@
         def __init__(self, buffer, k):
             self.buffer, self.k = buffer, k
             mine = buffer.at[rows_of(m, k)]
-            self.far = net.send(mine, mine, by_side)
-            self.near = net.send(mine, mine, by_core)
+            self.far = net.send(mine, mine, by_side, (k, 0))
+            self.near = net.send(mine, mine, by_core, (k, 1))
 
         def forward(self):
             self.far.wait_recv()
             there = self.buffer.at[rows_of(m2, self.k)]
-            self.passed = net.send(there, there, by_core)
+            self.passed = net.send(there, there, by_core, (self.k, 2))
 
         def finish(self):
             self.near.wait_recv()
@@ -419,29 +451,29 @@
             self.k = k
             for copy in Scatter.last.get(k, []):
                 net.sent(copy)
-            part = s.partial.at[k]
+            part = partial[k]
             self.near = []
             for r, model in ((0, m3), (1, m1)):
                 here = pl.ds(pl.multiple_of(model * BLOCK, BLOCK), BLOCK)
                 s.near_send[k, r] = part[here, :].astype(bf16)
                 self.near.append(
-                    net.send(s.near_send.at[k, r], s.near_land.at[k, r], by_core)
+                    net.send(s.near_send.at[k, r], s.near_land.at[k, r], by_core, (k, 3 + r))
                 )
 
         def middle(self):
             k = self.k
             self.near[0].wait_recv()
             here = pl.ds(pl.multiple_of(m2 * BLOCK, BLOCK), BLOCK)
-            total = s.partial[k, here, :] + s.near_land[k, 0].astype(f32)
+            total = partial[k][here, :] + s.near_land[k, 0].astype(f32)
             s.far_send[k] = total.astype(bf16)
-            self.far = net.send(s.far_send.at[k], s.far_land.at[k], by_side)
+            self.far = net.send(s.far_send.at[k], s.far_land.at[k], by_side, (k, 5))
             Scatter.last[k] = self.near + [self.far]
 
         def end(self):
             k = self.k
             self.near[1].wait_recv()
             here = pl.ds(pl.multiple_of(m * BLOCK, BLOCK), BLOCK)
-            total = s.partial[k, here, :] + s.near_land[k, 1].astype(f32)
+            total = partial[k][here, :] + s.near_land[k, 1].astype(f32)
             self.far.wait_recv()
             return total + s.far_land[k].astype(f32)
 
@@ -474,12 +506,12 @@
 
     def key_mask(model, k, is_long):
         if is_long:
-            return lane < long_ref[0, model * per_long + k]
+            return sub < long_ref[0, model * per_long + k]
         keep = None
         for j in range(short_in_block):
             size = short_ref[0, (model - long_blocks) * per_short + k * short_in_block + j]
             start = j * SHORT_LEN
-            ok = (lane >= start) & (lane < start + size) & (sub >= start) & (sub < start + SHORT_LEN)
+            ok = (sub >= start) & (sub < start + size) & (lane >= start) & (lane < start + SHORT_LEN)
             keep = ok if keep is None else keep | ok
         return keep
 
@@ -500,57 +532,92 @@
             outs = []
             for h in range(heads):
                 query = head_parts(proj, rows, h, 0) * head_masks[h % 2]
-                scores = nt(query, head_parts(proj, rows, h, 1)) * 0.125
+                scores = nt(head_parts(proj, rows, h, 1), query) * 0.125
                 scores = jnp.where(keep, scores, -1e30)
-                weights = jnp.exp(scores - jnp.max(scores, axis=1, keepdims=True))
-                weights = weights / jnp.sum(weights, axis=1, keepdims=True)
+                weights = jnp.exp(scores - jnp.max(scores, axis=0, keepdims=True))
+                weights = weights * (1.0 / jnp.sum(weights, axis=0, keepdims=True))
                 probs[k, model, h] = weights
-                outs.append(nn(weights.astype(bf16), head_parts(proj, rows, h, 2)))
+                outs.append(tn(weights.astype(bf16), head_parts(proj, rows, h, 2)))
             for g in range(pad // BLOCK):
                 second = outs[2 * g + 1] if 2 * g + 1 < heads else jnp.zeros((BLOCK, BLOCK), f32)
                 both = jnp.where(first_half, outs[2 * g], second)
                 att[rows, pl.ds(g * BLOCK, BLOCK)] = both.astype(bf16)
 
-        for is_long, low_model in ((True, 0), (False, long_blocks)):
-            def one(at, carry, is_long=is_long, low_model=low_model):
-                block(is_long, low_model + at)
-                return carry
-
-            lax.fori_loop(0, long_blocks, one, 0)
+        for model in range(n_model):
+            block(model < long_blocks, model)
 
         def mix(at):
             rows = pl.ds(pl.multiple_of(k * span + at, 256), 256)
-            s.partial[k, pl.ds(at, 256), :] = nn(att[rows, :], mixw[...])
+            partial[k][pl.ds(at, 256), :] = nn(att[rows, :], mixw[...])
 
         tiles(span, 256, mix)
 
-    def pipeline(gathers, work, before=None, after=None, forwarded=None):
+    nothing = ((),) * chunks
+
+    def pipeline(gathers, work, forward=nothing, middle=nothing, finish=nothing, also=None):
         scatters = []
         for k in range(chunks):
             if gathers:
+                steps(*forward[k])
                 gathers[k].forward()
-            if forwarded is not None:
-                forwarded(k)
             if k:
+                steps(*middle[k - 1])
                 scatters[k - 1].middle()
             if gathers:
+                steps(*finish[k])
                 gathers[k].finish()
-            if before is not None:
-                before(k)
+            if also is not None and k == chunks - 1:
+                also()
             work(k)
             scatters.append(Scatter(k))
-            if after is not None:
-                after(k)
+        steps(*middle[-1])
         scatters[-1].middle()
         return scatters
 
+    bits = tuple(range(n_data.bit_length() - 1))
+    part_rows = [width // 3] * 3 + [ff // 3] * 3 + [cols] * 4
+    part_at = [sum(part_rows[:i]) for i in range(len(part_rows))]
+    reduces = [
+        Reduce(
+            net,
+            s.grads.at[pl.ds(at, rows)],
+            sums.at[pl.ds(at, rows)],
+            s.sum_land.at[i],
+            (d, m),
+            bits,
+        )
+        for i, (at, rows) in enumerate(zip(part_at, part_rows, strict=True))
+    ]
+    norm_sum = s.norm_sum
+    norm_copies, norm_done = [], []
+    stages = [by_core, by_side] + [reduces[0].partner(bit)[1] for bit in bits]
+
+    def norm_send():
+        at = len(norm_copies)
+        if at < len(stages):
+            norm_copies.append(net.send(norm_sum.at[at], s.norm_land.at[at], stages[at]))
+
+    def norm_step():
+        at = len(norm_copies) - 1
+        norm_copies[at].wait_recv()
+        norm_sum[at + 1] = norm_sum[at] + s.norm_land[at]
+        norm_done.append(at)
+        norm_send()
+
+    def steps(*order):
+        for at in order:
+            if at == NORM:
+                norm_step()
+            else:
+                reduces[at].step()
+
     scatters = pipeline(gathers, attend)
 
     gain_one, shift_one, gain_two, shift_two = [
         ref[...].reshape(1, width)
-        for ref in (gain_one_ref, shift_one_ref, gain_two_ref, shift_two_ref)
+        for ref in (s.gain_one, s.shift_one, s.gain_two, s.shift_two)
     ]
-    norm, act, slope = s.norm, s.act, s.slope
+    norm, act = s.norm, s.act
     gathers = []
     for k in range(chunks):
         hidden = x[rows_of(m, k), :].astype(f32) + scatters[k].end()
@@ -574,7 +641,7 @@
 
         def two(at):
             rows = pl.ds(pl.multiple_of(k * span + at, 256), 256)
-            s.partial[k, pl.ds(at, 256), :] = nn(act[rows, :], downw[...])
+            partial[k][pl.ds(at, 256), :] = nn(act[rows, :], downw[...])
 
         tiles(span, 256, two)
 
@@ -614,8 +681,8 @@
         return pltpu.make_async_remote_copy(
             src_ref=pool.at[d, m],
             dst_ref=pool.at[d, m],
-            send_sem=s.pool_send.at[j],
-            recv_sem=s.pool_recv.at[j],
+            send_sem=s.pool_sems.at[0],
+            recv_sem=s.pool_sems.at[1],
             device_id=(lax.rem(d + j, n_data), m),
             device_id_type=MESH,
         )
@@ -624,16 +691,12 @@
         pool_copy(j).start()
         return carry
 
-    def pool_arrived(j, carry):
-        pool_copy(j).wait_recv()
-        return carry
-
-    def pool_sent(j, carry):
-        pool_copy(j).wait_send()
-        return carry
+    def pool_wait(at):
+        blocks = pool.at[pl.ds(0, n_data - 1), m]
+        pltpu.make_async_copy(blocks, blocks, s.pool_sems.at[at]).wait()
 
     lax.fori_loop(1, n_data, pool_start, 0)
-    lax.fori_loop(1, n_data, pool_arrived, 0)
+    pool_wait(1)
     far = net.send(pool.at[:, m], pool.at[:, m], by_side)
     near = net.send(pool.at[:, m], pool.at[:, m], by_core)
     far.wait_recv()
@@ -762,7 +825,6 @@
         grad_rows[at, :] = grad_rows[at, :] + grad_firsts[i : i + 1, :]
 
 
-    norm_sum = s.norm_sum
     norm_sum[0] = jnp.zeros((8, width), f32)
     for k in range(chunks):
         s.second[own_rows(k), :] = second_back(k)
@@ -814,7 +876,7 @@
 
         def two(at):
             rows = pl.ds(pl.multiple_of(k * span + at, 256), 256)
-            s.partial[k, pl.ds(at, 256), :] = nt(gp[rows, :], upw[...])
+            partial[k][pl.ds(at, 256), :] = nt(gp[rows, :], upw[...])
 
         tiles(span, 256, two)
 
@@ -827,44 +889,21 @@
 
         tiles(rows, step, one)
 
-    def whole_grad(target, base, left, right, keep=None):
-        total = left.shape[1]
-        for at in range(0, total, 256):
-            part = tn(left[:, at : at + 256], right[...]).astype(bf16)
-            size = 256 if keep is None else keep
-            target[pl.ds(base + (at // 256) * size, size), :] = part[:size]
-
-    bits = tuple(range(n_data.bit_length() - 1))
-    half_rows = width // 2
-    reduces = [
-        Reduce(
-            net,
-            s.grads.at[pl.ds(i * half_rows, half_rows)],
-            s.sums.at[pl.ds(i * half_rows, half_rows)],
-            s.sum_land.at[i],
-            (d, m),
-            bits,
-        )
-        for i in range(6)
-    ]
-    downs, ups, heads_sums = reduces[0:2], reduces[2:4], reduces[4:6]
-
-    def steps(*order):
-        for at in order:
-            reduces[at].step()
-
-    def begin(items, base, left, right):
-        for i, item in enumerate(items):
-            for at in range(i * half_rows, (i + 1) * half_rows, half_rows):
-                part = tn(left[:, at : at + half_rows], right[...])
-                s.grads[pl.ds(base + at, half_rows), :] = part.astype(bf16)
+    def begin(first, left, right, step):
+        for i, at in enumerate(range(0, left.shape[1], step)):
+            item = reduces[first + i]
+            part = tn(left[:, at : at + step], right[...]).astype(bf16)
+            here = pl.ds(part_at[first + i], part_rows[first + i])
+            s.grads[here, :] = part[: part_rows[first + i]]
             item.start()
 
-    begin(downs, 0, act, gb)
-    scatters = pipeline([], feed_back)
-    begin(ups, width, norm, gp)
+    begin(0, act, gb, part_rows[0])
+    scatters = pipeline([], feed_back, middle=((), (0,)))
+    begin(3, norm, gp, part_rows[3])
+    before_end = ((1,), (0, 2, 1))
     gathers = []
     for k in range(chunks):
+        steps(*before_end[k])
         grad = s.second[own_rows(k), :] + scatters[k].end()
         normal = s.normal_one[own_rows(k), :]
         norm_sum[0, 0:1, :] = norm_sum[0, 0:1, :] + jnp.sum(grad * normal, axis=0, keepdims=True)
@@ -873,7 +912,7 @@
         s.second[own_rows(k), :] = back
         gm[rows_of(m, k), :] = back.astype(bf16)
         gathers.append(Gather(gm, k))
-        steps(0)
+    norm_send()
 
     def attend_back(k):
         def unmix(at):
@@ -882,7 +921,7 @@
 
         tiles(span, 256, unmix)
 
-        def block(model, carry):
+        def block(model):
             rows = rows_of(model, k)
             parts = ([], [], [])
             for h in range(heads):
@@ -890,12 +929,12 @@
                 mask = head_masks[h % 2]
                 grad_out = s.gatt[rows, pl.ds(g * BLOCK, BLOCK)] * mask
                 weights = probs[k, model, h]
-                grad_probs = nt(grad_out, head_parts(proj, rows, h, 2))
-                inner = jnp.sum(weights * grad_probs, axis=1, keepdims=True)
+                grad_probs = nt(head_parts(proj, rows, h, 2), grad_out)
+                inner = jnp.sum(weights * grad_probs, axis=0, keepdims=True)
                 grad_scores = (weights * (grad_probs - inner)).astype(bf16)
-                parts[0].append(nn(grad_scores, head_parts(proj, rows, h, 1)) * 0.125)
-                parts[1].append(tn(grad_scores, head_parts(proj, rows, h, 0)) * 0.125)
-                parts[2].append(tn(weights.astype(bf16), grad_out))
+                parts[0].append(tn(grad_scores, head_parts(proj, rows, h, 1)) * 0.125)
+                parts[1].append(nn(grad_scores, head_parts(proj, rows, h, 0)) * 0.125)
+                parts[2].append(nn(weights.astype(bf16), grad_out))
             for part in range(3):
                 for g in range(pad // BLOCK):
                     outs = parts[part]
@@ -903,37 +942,30 @@
                     second = outs[2 * g + 1] if 2 * g + 1 < heads else zero
                     both = jnp.where(first_half, outs[2 * g], second)
                     gproj[rows, pl.ds(part * pad + g * BLOCK, BLOCK)] = both.astype(bf16)
-            return carry
-
-        lax.fori_loop(0, n_model, block, 0)
+
+        for model in range(n_model):
+            block(model)
 
         def one(at):
             rows = pl.ds(pl.multiple_of(k * span + at, 256), 256)
-            s.partial[k, pl.ds(at, 256), :] = nn(gproj[rows, :], wt[...])
+            partial[k][pl.ds(at, 256), :] = nn(gproj[rows, :], wt[...])
 
         tiles(span, 256, one)
 
-    def forwarded(k):
-        if k == 0:
-            steps(1)
-
-    def before_attend(k):
-        if k == chunks - 1:
-            steps(2)
-
-    def after_attend(k):
-        if k == 0:
-            steps(0, 1)
-
-    scatters = pipeline(gathers, attend_back, before_attend, after_attend, forwarded)
-    steps(0, 1, 2)
-    whole_grad(s.grads, 2 * width, att, gm, cols)
-    whole_grad(s.grads, 2 * width + cols, gproj, x, cols)
-    for item in heads_sums:
-        item.start()
-    steps(3, 0, 2, 1)
+    scatters = pipeline(
+        gathers,
+        attend_back,
+        forward=((0, 3, 2, NORM), (0, 4, 3, 2, NORM)),
+        middle=((), (NORM, 0, 4)),
+        finish=((1,), (1, 5)),
+        also=lambda: begin(6, att, gm, pad),
+    )
+    begin(7, gproj, x, pad)
+    steps(6, 3, 2)
+    before_end = ((), (1, 0, 5, NORM))
     swap_sent(s.returned, row_sems)
     for k in range(chunks):
+        steps(*before_end[k])
         grad = s.second[own_rows(k), :] + scatters[k].end()
         s.grad_in[own_rows(k), :] = grad.astype(bf16)
 
@@ -944,41 +976,118 @@
     tiles(slots, 256, pack)
     swap_start(s.outgoing, s.incoming, out_sems)
 
-    stages = [by_core, by_side]
-    for bit in bits:
-        stages.append(reduces[0].partner(bit)[1])
-
-    def norm_step(at):
-        copy = net.send(norm_sum.at[at], s.norm_land.at[at], stages[at])
-        copy.wait_recv()
-        norm_sum[at + 1] = norm_sum[at] + s.norm_land[at]
-
-    order = [3, 1, 2, 3, 4, 2, 4, 5, 3, 4, 5, 3, 0, 1, 4, 5, 2, 4, 5, 3, 5, 4, 5]
-    turn = 0
-    while turn < len(stages) or any(item.todo for item in reduces):
-        if turn < len(stages):
-            norm_step(turn)
-        if not order:
-            order = [i for i, item in enumerate(reduces) if item.todo]
-        for at in order[:4]:
-            if reduces[at].todo:
-                steps(at)
-        order = order[4:]
-        turn += 1
+    tail = [4, 7, 6, 3, NORM, 8, 2, 5, 9, 1, 7, 4, 3, 2, 6, 8, 5, 9, 7, 3, 4]
+    rest_of_tail = [6, 8, 5, 9, 7, 4, 6, 8, 9, 7, 5, 8, 9, 6, 7, 8, 9]
+    if resident:
+        moments = [
+            pltpu.make_async_copy(first_hbm, first_out, s.load_sems.at[0]),
+            pltpu.make_async_copy(second_hbm, second_out, s.load_sems.at[1]),
+        ]
+        for copy in moments:
+            copy.start()
+    steps(*tail)
+    swap_arrived(s.incoming, out_sems)
+    if resident:
+        for copy in moments:
+            copy.wait()
+        rows = table_rows // 8
+        for at in range(8):
+            here = pl.ds(at * rows, rows)
+            first_new, second_new, step = table_update(
+                s.ids[0:1, :],
+                s.incoming[...],
+                first_out[here, :],
+                second_out[here, :],
+                step_out[here, :],
+                at * rows,
+            )
+            first_out[here, :] = first_new
+            second_out[here, :] = second_new
+            step_out[here, :] = step
+            steps(*rest_of_tail[2 * at : 2 * at + 2])
+        rest_of_tail = rest_of_tail[16:]
+    steps(*rest_of_tail)
+    while any(item.todo for item in reduces):
+        steps(*(i for i, item in enumerate(reduces) if item.todo))
+    while len(norm_done) < len(stages):
+        norm_step()
     norm_out[...] = norm_sum[len(stages)]
-    swap_arrived(s.incoming, out_sems)
-    outs = [
-        pltpu.make_async_copy(s.sums, weight_out, s.load_sems.at[0]),
-        pltpu.make_async_copy(s.incoming, incoming_out, s.load_sems.at[1]),
-    ]
-    for copy in outs:
-        copy.start()
-    for copy in outs:
-        copy.wait()
+    if not resident:
+        outs = [
+            pltpu.make_async_copy(sums, weight_out, s.load_sems.at[0]),
+            pltpu.make_async_copy(s.incoming, incoming_out, s.load_sems.at[1]),
+            pltpu.make_async_copy(s.ids, ids_hbm, s.load_sems.at[2]),
+        ]
+        for copy in outs:
+            copy.start()
+        for copy in outs:
+            copy.wait()
     net.drain()
-    lax.fori_loop(1, n_data, pool_sent, 0)
+    pool_wait(0)
     swap_sent(s.asked, ask_sems)
     swap_sent(s.incoming, out_sems)
+
+
+def table_update(ids, incoming, first, second, table, base):
+    rows, slots = first.shape[0], incoming.shape[0]
+    hot = (iota((rows, slots), 0) + base == ids).astype(f32)
+    uses = jnp.sum(hot, axis=1, keepdims=True)
+    row_grad = nn(hot.astype(bf16), incoming) * (1.0 / jnp.maximum(uses, 1.0))
+    first_new = 0.9 * first + 0.1 * row_grad
+    second_new = 0.95 * second + 0.05 * row_grad * row_grad
+    scale = jnp.sqrt(second_new * (1.0 / second_fix)) + 1e-08
+    return first_new, second_new, first_new * (1.0 / first_fix) / scale + 0.01 * table
+
+
+def finish_kernel(
+    cols,
+    norm_ref,
+    loss_ref,
+    low,
+    step_ref,
+    first_ref,
+    second_ref,
+    step_hbm,
+    first_out,
+    second_out,
+    down_out,
+    up_out,
+    mix_out,
+    heads_out,
+    loss_out,
+    *rest,
+):
+    norm_outs = rest[:4]
+    wide, state_sems, wide_sems = rest[4:]
+    width = low.shape[1]
+    states = [
+        pltpu.make_async_copy(src, dst, state_sems.at[i])
+        for i, (src, dst) in enumerate(
+            ((step_ref, step_hbm), (first_ref, first_out), (second_ref, second_out))
+        )
+    ]
+    for copy in states:
+        copy.start()
+    loss_out[...] = loss_ref[0:1, 0:1]
+    for i, out in enumerate(norm_outs):
+        out[...] = norm_ref[i, :]
+    starts = (0, width, 2 * width, 2 * width + cols, 3 * width)
+    wides = []
+    for i, out in enumerate((down_out, up_out, mix_out, heads_out)):
+        count = starts[i + 1] - starts[i]
+        here = pl.ds(starts[i], count)
+        step = 96
+
+        def one(at, carry, base=starts[i]):
+            rows = pl.ds(pl.multiple_of(base + at * step, 16), step)
+            wide[rows, :] = low[rows, :].astype(f32)
+            return carry
+
+        lax.fori_loop(0, count // step, one, 0)
+        wides.append(pltpu.make_async_copy(wide.at[here], out, wide_sems.at[i]))
+        wides[-1].start()
+    for copy in states + wides:
+        copy.wait()
 
 
 def table_kernel(
@@ -1073,15 +1182,17 @@
         for i in range(3):
             load(i, at).wait()
         here = tile(at)
-        hot = (iota((rows, slots), 0) + at * rows == ids_ref[0:1, :]).astype(f32)
-        uses = jnp.sum(hot, axis=1, keepdims=True)
-        row_grad = nn(hot.astype(bf16), incoming[...]) * (1.0 / jnp.maximum(uses, 1.0))
-        first_new = 0.9 * state[0, here, :] + 0.1 * row_grad
-        second_new = 0.95 * state[1, here, :] + 0.05 * row_grad * row_grad
+        first_new, second_new, step = table_update(
+            ids_ref[0:1, :],
+            incoming[...],
+            state[0, here, :],
+            state[1, here, :],
+            state[2, here, :],
+            at * rows,
+        )
         state[0, here, :] = first_new
         state[1, here, :] = second_new
-        scale = jnp.sqrt(second_new * (1.0 / second_fix)) + 1e-08
-        state[2, here, :] = first_new * (1.0 / first_fix) / scale + 0.01 * state[2, here, :]
+        state[2, here, :] = step
         for i in range(3):
             store(i, at).start()
         return carry
@@ -1127,11 +1238,9 @@
     firsts = devices * per_short
     table_rows = embed_table.shape[0]
     bits = n_data.bit_length() - 1
-    n_sems = 96 + 16 * bits
     vmem = pltpu.VMEM
     dma = pltpu.SemaphoreType.DMA
     shapes = dict(
-        stage=vmem((chunks, span, width), f32),
         table=vmem((table_rows, width), bf16),
         wt=vmem((3 * pad, width), bf16),
         mixw=vmem((pad, width), bf16),
@@ -1153,16 +1262,10 @@
         near_land=vmem((chunks, 2, BLOCK, width), bf16),
         far_send=vmem((chunks, BLOCK, width), bf16),
         far_land=vmem((chunks, BLOCK, width), bf16),
-        normal_one=vmem((tok, width), f32),
         scale_one=vmem((tok, 128), f32),
-        normed=vmem((tok, width), f32),
         norm=vmem((group, width), bf16),
         act=vmem((group, ff), bf16),
-        slope=vmem((group, ff), f32),
-        normal_two=vmem((tok, width), f32),
         scale_two=vmem((tok, 128), f32),
-        rows=vmem((tok, width), f32),
-        grad_rows=vmem((tok, width), f32),
         patch=vmem((n_model, 2 * per_short, width // 2), bf16),
         pool=vmem((n_data, n_model, 2 * per_short, width // 2), bf16),
         left=vmem((firsts, width // 2), bf16),
@@ -1172,26 +1275,40 @@
         known_col=vmem((firsts, 128), f32),
         gb=vmem((group, width), bf16),
         gm=vmem((group, width), bf16),
-        second=vmem((tok, width), f32),
         grad_in=vmem((tok, width), bf16),
         norm_sum=vmem((3 + bits, 8, width), f32),
         norm_land=vmem((2 + bits, 8, width), f32),
         grads=vmem((3 * width, width), bf16),
-        sums=vmem((3 * width, width), bf16),
-        sum_land=vmem((6, width, width // 2), bf16),
-        send_sems=dma((n_sems,)),
-        recv_sems=dma((n_sems,)),
-        load_sems=dma((16,)),
-        ask_send=dma((devices,)),
-        ask_recv=dma((devices,)),
-        row_send=dma((devices,)),
-        row_recv=dma((devices,)),
-        out_send=dma((devices,)),
-        out_recv=dma((devices,)),
-        pool_send=dma((n_data,)),
-        pool_recv=dma((n_data,)),
+        sum_land=vmem((10, 3 * width // 4, width // 2), bf16),
+        send_sems=dma((32,)),
+        recv_sems=dma((20 + 21 * bits,)),
+        owner=vmem((1, group), i32),
+        rowid=vmem((1, group), i32),
+        long=pltpu.SMEM(long_len.shape, i32),
+        short=pltpu.SMEM(short_len.shape, i32),
+        pairing=vmem((1, pairing.shape[0]), i32),
+        gain_one=vmem((width,), f32),
+        shift_one=vmem((width,), f32),
+        gain_two=vmem((width,), f32),
+        shift_two=vmem((width,), f32),
+        small_sems=dma((9,)),
+        load_sems=dma((8,)),
+        table_sems=dma((max(4, table_rows // span),)),
+        ids=vmem((8, slots), i32),
+        ask_sems=dma((2,)),
+        row_sems=dma((2,)),
+        out_sems=dma((2,)),
+        pool_sems=dma((2,)),
     )
+    resident = devices <= 32
+    if not resident:
+        shapes.update(
+            wide_a=vmem((2 * group, width), f32),
+            wide_b=vmem((6 * tok, width), f32),
+            sums=vmem((3 * width, width), bf16),
+        )
     dims = SimpleNamespace(
+        resident=resident,
         n_data=n_data,
         n_model=n_model,
         names=tuple(shapes),
@@ -1204,24 +1321,35 @@
         shorts=short_len.shape[1],
     )
     in_vmem = pl.BlockSpec(memory_space=pltpu.VMEM)
-    in_smem = pl.BlockSpec(memory_space=pltpu.SMEM)
     in_hbm = pl.BlockSpec(memory_space=pl.ANY)
     heads_rows = jnp.transpose(heads_weight, (1, 2, 0)).reshape(3 * cols, width)
-    block_out, weights, norms, loss, incoming, ids = pl.pallas_call(
-        functools.partial(layer_kernel, dims),
-        out_shape=(
-            jax.ShapeDtypeStruct((tok, width), bf16),
+    whole = jax.ShapeDtypeStruct((table_rows, width), f32)
+    out_shape = (
+        jax.ShapeDtypeStruct((tok, width), bf16),
+        jax.ShapeDtypeStruct((8, width), f32),
+        jax.ShapeDtypeStruct((8, 128), f32),
+    )
+    if resident:
+        out_shape = out_shape[:1] + (vmem((8, width), f32), vmem((8, 128), f32))
+        out_shape += (vmem((3 * width, width), bf16),) + (vmem((table_rows, width), f32),) * 3
+        out_specs = (in_vmem,) * 7
+    else:
+        out_shape += (
             jax.ShapeDtypeStruct((3 * width, width), bf16),
-            jax.ShapeDtypeStruct((8, width), f32),
-            jax.ShapeDtypeStruct((8, 128), f32),
             jax.ShapeDtypeStruct((slots, width), bf16),
             jax.ShapeDtypeStruct((8, slots), i32),
-        ),
-        in_specs=[in_vmem, in_vmem, in_smem, in_smem] + [in_vmem] * 5 + [in_hbm] * 6,
-        out_specs=(in_vmem, in_hbm, in_vmem, in_vmem, in_hbm, in_vmem),
+        )
+        out_specs = (in_vmem,) * 3 + (in_hbm,) * 3
+    block_out, norms, loss, *more = pl.pallas_call(
+        functools.partial(layer_kernel, dims),
+        out_shape=out_shape,
+        in_specs=[in_hbm] * 17,
+        out_specs=out_specs,
         scratch_shapes=list(shapes.values()),
         compiler_params=pltpu.CompilerParams(
-            collective_id=0, has_side_effects=True, vmem_limit_bytes=63 * 2**20
+            collective_id=0,
+            has_side_effects=True,
+            vmem_limit_bytes=(40 if resident else 63) * 2**20,
         ),
     )(
         token_owner.reshape(1, group),
@@ -1239,20 +1367,33 @@
         up_weight,
         down_weight,
         upper_grad,
+        first_moment,
+        second_moment,
     )
-    parts = 8
-    whole = jax.ShapeDtypeStruct((table_rows, width), f32)
-    table_step, first_new, second_new, down_grad, up_grad, mix_grad, heads_grad, loss, *norm_grads = (
-        pl.pallas_call(
+    out_shape = (
+        (whole, whole, whole)
+        + tuple(jax.ShapeDtypeStruct((rows, width), f32) for rows in (ff, width, cols, 3 * cols))
+        + (jax.ShapeDtypeStruct((1, 1), f32),)
+        + (jax.ShapeDtypeStruct((width,), f32),) * 4
+    )
+    out_specs = (in_hbm,) * 7 + (in_vmem,) * 5
+    if resident:
+        finished = pl.pallas_call(
+            functools.partial(finish_kernel, cols),
+            out_shape=out_shape,
+            in_specs=[in_vmem] * 6,
+            out_specs=out_specs,
+            scratch_shapes=[vmem((3 * width, width), f32), dma((3,)), dma((4,))],
+            compiler_params=pltpu.CompilerParams(vmem_limit_bytes=20 * 2**20),
+        )(norms, loss, *more)
+    else:
+        weights, incoming, ids = more
+        parts = 8
+        finished = pl.pallas_call(
             functools.partial(table_kernel, cols),
-            out_shape=(whole, whole, whole)
-            + tuple(
-                jax.ShapeDtypeStruct((rows, width), f32) for rows in (ff, width, cols, 3 * cols)
-            )
-            + (jax.ShapeDtypeStruct((1, 1), f32),)
-            + (jax.ShapeDtypeStruct((width,), f32),) * 4,
+            out_shape=out_shape,
             in_specs=[in_vmem] * 3 + [in_hbm] * 5,
-            out_specs=(in_hbm,) * 7 + (in_vmem,) * 5,
+            out_specs=out_specs,
             scratch_shapes=[
                 vmem((slots, width), bf16),
                 vmem((3 * width, width), bf16),
@@ -1265,7 +1406,8 @@
             ],
             compiler_params=pltpu.CompilerParams(vmem_limit_bytes=63 * 2**20),
         )(ids, norms, loss, incoming, weights, embed_table, first_moment, second_moment)
-    )
+    table_step, first_new, second_new, down_grad, up_grad, mix_grad, heads_grad, loss = finished[:8]
+    norm_grads = finished[8:]
     return (
         loss.reshape(()),
         block_out,

time: 240 us -> 208 us (0.87)
  Pallas kernels: 238 us -> 207 us
    pallas_call x2, Pallas kernels: 238 us -> 207 us  [the longest x1 197 us: body(): pl.pallas_call(functools.partial(layer_kernel, dims), out_shape=out_shape...]
where the time goes in v2:
time: 208 us
  Pallas kernels  207 us (100%)
    pallas_call x1, Pallas kernels, body(): pl.pallas_call(functools.partial(layer_kernel, dims), out_shape=out_shape...  197 us
    pallas_call x1, Pallas kernels, body(): pl.pallas_call(functools.partial(finish_kernel, cols), out_shape=out_shap...  9.32 us

profile of v2, /device:TPU:0, one launch (start us, length us, event | category | flops | bytes accessed | tf_op | source)
XLA Modules:
  0.0 208.0 jit_solution(13891077353488396275)
XLA Ops:
  0.7 197.2 %shard_map.264 = (bf16[256,768]{1,0:T(8,128)(2,1)}, f32[8,768]{1,0:T(8,128)S(1)}, f32[8,128]{1,0:T(8,128)S(1)}, bf16[2304,768]{1,0:T(8,128)(2,1)S(1)}, f32[2048,...) custom-call(s32[1,1024]{1,0:T(1,128)} %bitcast.11, s32[1,1024]{1,0:T(1,128)} %bitcast.12, ...), custom_call_target="tpu_custom_call" | custom-call | tf_op jit(solution)/shard_map/pallas_call | solution.py:1343
  197.9 0.0 copy-start
  197.9 9.3 %shard_map.265 = (f32[2048,768]{1,0:T(8,128)}, f32[2048,768]{1,0:T(8,128)}, f32[2048,768]{1,0:T(8,128)}, f32[768,768]{1,0:T(8,128)}, f32[768,768]{1,0:T(8,128)},...) custom-call(f32[8,768]{1,0:T(8,128)S(1)} %get-tuple-element.32.norm_, ...), custom_call_target="tpu_custom_call" | custom-call | tf_op jit(solution)/shard_map/pallas_call | solution.py:1381
  207.2 0.0 copy-done
  207.2 0.7 copy.31
Async XLA Ops:
  197.9 9.3 %copy-start = (bf16[256,768]{1,0:T(8,128)(2,1)S(1)}, bf16[256,768]{1,0:T(8,128)(2,1)}, u32[]{:S(2)}) copy-start(bf16[256,768]{1,0:T(8,128)(2,1)} %get-tuple-element.65) | copy-start | bytes 1179652

commit v3 on v2

--- a/solution.py
+++ b/solution.py
@@ -521,36 +521,42 @@
 
     def attend(k):
         def project(at):
-            rows = pl.ds(pl.multiple_of(k * span + at, 256), 256)
+            rows = pl.ds(pl.multiple_of(k * span + at, 512), 512)
             proj[rows, :] = nt(x[rows, :], wt[...]).astype(bf16)
 
-        tiles(span, 256, project)
-
-        def block(is_long, model):
+        tiles(span, 512, project)
+
+        units = [(model, h) for model in range(n_model) for h in range(heads)]
+        keeps = [key_mask(model, k, model < long_blocks) for model in range(n_model)]
+        scores = []
+        for model, h in units:
             rows = rows_of(model, k)
-            keep = key_mask(model, k, is_long)
-            outs = []
-            for h in range(heads):
-                query = head_parts(proj, rows, h, 0) * head_masks[h % 2]
-                scores = nt(head_parts(proj, rows, h, 1), query) * 0.125
-                scores = jnp.where(keep, scores, -1e30)
-                weights = jnp.exp(scores - jnp.max(scores, axis=0, keepdims=True))
-                weights = weights * (1.0 / jnp.sum(weights, axis=0, keepdims=True))
-                probs[k, model, h] = weights
-                outs.append(tn(weights.astype(bf16), head_parts(proj, rows, h, 2)))
+            query = head_parts(proj, rows, h, 0) * head_masks[h % 2]
+            scores.append(nt(head_parts(proj, rows, h, 1), query))
+        weights = []
+        for (model, h), score in zip(units, scores, strict=True):
+            score = jnp.where(keeps[model], score * 0.125, -1e30)
+            part = jnp.exp(score - jnp.max(score, axis=0, keepdims=True))
+            weights.append(part * (1.0 / jnp.sum(part, axis=0, keepdims=True)))
+        outs = {}
+        for unit, weight in zip(units, weights, strict=True):
+            value = head_parts(proj, rows_of(unit[0], k), unit[1], 2)
+            outs[unit] = tn(weight.astype(bf16), value)
+        for unit, weight in zip(units, weights, strict=True):
+            probs[(k, *unit)] = weight
+        for model in range(n_model):
             for g in range(pad // BLOCK):
-                second = outs[2 * g + 1] if 2 * g + 1 < heads else jnp.zeros((BLOCK, BLOCK), f32)
-                both = jnp.where(first_half, outs[2 * g], second)
-                att[rows, pl.ds(g * BLOCK, BLOCK)] = both.astype(bf16)
-
-        for model in range(n_model):
-            block(model < long_blocks, model)
+                second = outs.get((model, 2 * g + 1))
+                if second is None:
+                    second = jnp.zeros((BLOCK, BLOCK), f32)
+                both = jnp.where(first_half, outs[model, 2 * g], second)
+                att[rows_of(model, k), pl.ds(g * BLOCK, BLOCK)] = both.astype(bf16)
 
         def mix(at):
-            rows = pl.ds(pl.multiple_of(k * span + at, 256), 256)
-            partial[k][pl.ds(at, 256), :] = nn(att[rows, :], mixw[...])
-
-        tiles(span, 256, mix)
+            rows = pl.ds(pl.multiple_of(k * span + at, 512), 512)
+            partial[k][pl.ds(at, 512), :] = nn(att[rows, :], mixw[...])
+
+        tiles(span, 512, mix)
 
     nothing = ((),) * chunks
 
@@ -575,7 +581,7 @@
         return scatters
 
     bits = tuple(range(n_data.bit_length() - 1))
-    part_rows = [width // 3] * 3 + [ff // 3] * 3 + [cols] * 4
+    part_rows = [ff // 4] * 4 + [width // 4] * 4 + [cols] * 4
     part_at = [sum(part_rows[:i]) for i in range(len(part_rows))]
     reduces = [
         Reduce(
@@ -631,19 +637,19 @@
 
     def feed(k):
         def one(at):
-            rows = pl.ds(pl.multiple_of(k * span + at, 128), 128)
+            rows = pl.ds(pl.multiple_of(k * span + at, 512), 512)
             pre = nn(norm[rows, :], upw[...])
             cumulative = 0.5 * (1.0 + lax.erf(pre * 0.7071067811865476))
             act[rows, :] = (pre * cumulative).astype(bf16)
             slope[rows, :] = cumulative + pre * (0.3989422804014327 * jnp.exp(-0.5 * pre * pre))
 
-        tiles(span, 128, one)
+        tiles(span, 512, one)
 
         def two(at):
-            rows = pl.ds(pl.multiple_of(k * span + at, 256), 256)
-            partial[k][pl.ds(at, 256), :] = nn(act[rows, :], downw[...])
-
-        tiles(span, 256, two)
+            rows = pl.ds(pl.multiple_of(k * span + at, 512), 512)
+            partial[k][pl.ds(at, 512), :] = nn(act[rows, :], downw[...])
+
+        tiles(span, 512, two)
 
     scatters = pipeline(gathers, feed)
 
@@ -869,16 +875,16 @@
 
     def feed_back(k):
         def one(at):
-            rows = pl.ds(pl.multiple_of(k * span + at, 128), 128)
+            rows = pl.ds(pl.multiple_of(k * span + at, 512), 512)
             gp[rows, :] = (nt(gb[rows, :], downw[...]) * slope[rows, :]).astype(bf16)
 
-        tiles(span, 128, one)
+        tiles(span, 512, one)
 
         def two(at):
-            rows = pl.ds(pl.multiple_of(k * span + at, 256), 256)
-            partial[k][pl.ds(at, 256), :] = nt(gp[rows, :], upw[...])
-
-        tiles(span, 256, two)
+            rows = pl.ds(pl.multiple_of(k * span + at, 512), 512)
+            partial[k][pl.ds(at, 512), :] = nt(gp[rows, :], upw[...])
+
+        tiles(span, 512, two)
 
     def weight_grad(target, base, rows, left, right, left_at=0):
         step = 64
@@ -889,18 +895,21 @@
 
         tiles(rows, step, one)
 
-    def begin(first, left, right, step):
-        for i, at in enumerate(range(0, left.shape[1], step)):
-            item = reduces[first + i]
-            part = tn(left[:, at : at + step], right[...]).astype(bf16)
-            here = pl.ds(part_at[first + i], part_rows[first + i])
-            s.grads[here, :] = part[: part_rows[first + i]]
-            item.start()
-
-    begin(0, act, gb, part_rows[0])
+    def begin(first, last, left, right, keep=None):
+        base = made = part_at[first]
+        for at in range(0, left.shape[1], 256):
+            part = tn(left[:, at : at + 256], right[...]).astype(bf16)
+            count = 256 if keep is None else keep
+            s.grads[pl.ds(made, count), :] = part[:count]
+            made += count
+            while first < last and part_at[first] + part_rows[first] <= made:
+                reduces[first].start()
+                first += 1
+
+    begin(0, 4, act, gb)
     scatters = pipeline([], feed_back, middle=((), (0,)))
-    begin(3, norm, gp, part_rows[3])
-    before_end = ((1,), (0, 2, 1))
+    begin(4, 8, norm, gp)
+    before_end = ((1, 0), (2, 1, 0))
     gathers = []
     for k in range(chunks):
         steps(*before_end[k])
@@ -913,56 +922,62 @@
         gm[rows_of(m, k), :] = back.astype(bf16)
         gathers.append(Gather(gm, k))
     norm_send()
+    steps(3, 2)
 
     def attend_back(k):
         def unmix(at):
-            rows = pl.ds(pl.multiple_of(k * span + at, 256), 256)
+            rows = pl.ds(pl.multiple_of(k * span + at, 512), 512)
             s.gatt[rows, :] = nt(gm[rows, :], mixw[...]).astype(bf16)
 
-        tiles(span, 256, unmix)
-
-        def block(model):
+        tiles(span, 512, unmix)
+
+        units = [(model, h) for model in range(n_model) for h in range(heads)]
+        grads_out, grads_probs = [], []
+        for model, h in units:
             rows = rows_of(model, k)
-            parts = ([], [], [])
-            for h in range(heads):
-                g = h // 2
-                mask = head_masks[h % 2]
-                grad_out = s.gatt[rows, pl.ds(g * BLOCK, BLOCK)] * mask
-                weights = probs[k, model, h]
-                grad_probs = nt(head_parts(proj, rows, h, 2), grad_out)
-                inner = jnp.sum(weights * grad_probs, axis=0, keepdims=True)
-                grad_scores = (weights * (grad_probs - inner)).astype(bf16)
-                parts[0].append(tn(grad_scores, head_parts(proj, rows, h, 1)) * 0.125)
-                parts[1].append(nn(grad_scores, head_parts(proj, rows, h, 0)) * 0.125)
-                parts[2].append(nn(weights.astype(bf16), grad_out))
+            grad_out = s.gatt[rows, pl.ds((h // 2) * BLOCK, BLOCK)] * head_masks[h % 2]
+            grads_out.append(grad_out)
+            grads_probs.append(nt(head_parts(proj, rows, h, 2), grad_out))
+        lows, grads_scores = [], []
+        for unit, grad_probs in zip(units, grads_probs, strict=True):
+            weight = probs[(k, *unit)]
+            inner = jnp.sum(weight * grad_probs, axis=0, keepdims=True)
+            lows.append(weight.astype(bf16))
+            grads_scores.append((weight * (grad_probs - inner)).astype(bf16))
+        outs = {}
+        for i, (model, h) in enumerate(units):
+            rows = rows_of(model, k)
+            outs[0, model, h] = tn(grads_scores[i], head_parts(proj, rows, h, 1)) * 0.125
+            outs[1, model, h] = nn(grads_scores[i], head_parts(proj, rows, h, 0)) * 0.125
+            outs[2, model, h] = nn(lows[i], grads_out[i])
+        for model in range(n_model):
             for part in range(3):
                 for g in range(pad // BLOCK):
-                    outs = parts[part]
-                    zero = jnp.zeros((BLOCK, BLOCK), f32)
-                    second = outs[2 * g + 1] if 2 * g + 1 < heads else zero
-                    both = jnp.where(first_half, outs[2 * g], second)
-                    gproj[rows, pl.ds(part * pad + g * BLOCK, BLOCK)] = both.astype(bf16)
-
-        for model in range(n_model):
-            block(model)
+                    second = outs.get((part, model, 2 * g + 1))
+                    if second is None:
+                        second = jnp.zeros((BLOCK, BLOCK), f32)
+                    both = jnp.where(first_half, outs[part, model, 2 * g], second)
+                    gproj[rows_of(model, k), pl.ds(part * pad + g * BLOCK, BLOCK)] = both.astype(
+                        bf16
+                    )
 
         def one(at):
-            rows = pl.ds(pl.multiple_of(k * span + at, 256), 256)
-            partial[k][pl.ds(at, 256), :] = nn(gproj[rows, :], wt[...])
-
-        tiles(span, 256, one)
+            rows = pl.ds(pl.multiple_of(k * span + at, 512), 512)
+            partial[k][pl.ds(at, 512), :] = nn(gproj[rows, :], wt[...])
+
+        tiles(span, 512, one)
 
     scatters = pipeline(
         gathers,
         attend_back,
-        forward=((0, 3, 2, NORM), (0, 4, 3, 2, NORM)),
-        middle=((), (NORM, 0, 4)),
-        finish=((1,), (1, 5)),
-        also=lambda: begin(6, att, gm, pad),
+        forward=((1, NORM, 4, 0), (2, 5, 1, 4)),
+        middle=((NORM, 0, 6), (3, 2, 5, 7, NORM)),
+        finish=((3,), ()),
+        also=lambda: begin(8, 9, att, gm, cols),
     )
-    begin(7, gproj, x, pad)
-    steps(6, 3, 2)
-    before_end = ((), (1, 0, 5, NORM))
+    begin(9, 12, gproj, x, cols)
+    steps(1, 4, 6, 0)
+    before_end = ((), (3, 2, 8, 5))
     swap_sent(s.returned, row_sems)
     for k in range(chunks):
         steps(*before_end[k])
@@ -976,8 +991,9 @@
     tiles(slots, 256, pack)
     swap_start(s.outgoing, s.incoming, out_sems)
 
-    tail = [4, 7, 6, 3, NORM, 8, 2, 5, 9, 1, 7, 4, 3, 2, 6, 8, 5, 9, 7, 3, 4]
-    rest_of_tail = [6, 8, 5, 9, 7, 4, 6, 8, 9, 7, 5, 8, 9, 6, 7, 8, 9]
+    tail = [7, NORM, 9, 4, 6, 3, 10, 8, 5, 11, 1, 2, 9, 7, NORM, 4, 6, 10, 3]
+    rest_of_tail = [8, 5, 11, 4, 9, 7, 6, 5, 10, 8, 11, 9, 7, 6, 10, 8]
+    rest_of_tail += [11, 9, 7, 10, 11, 8, 9, 10, 11]
     if resident:
         moments = [
             pltpu.make_async_copy(first_hbm, first_out, s.load_sems.at[0]),
@@ -1041,6 +1057,7 @@
 
 def finish_kernel(
     cols,
+    block_ref,
     norm_ref,
     loss_ref,
     low,
@@ -1057,13 +1074,18 @@
     loss_out,
     *rest,
 ):
-    norm_outs = rest[:4]
-    wide, state_sems, wide_sems = rest[4:]
+    norm_outs, block_out = rest[:4], rest[4]
+    wide, state_sems, wide_sems = rest[5:]
     width = low.shape[1]
     states = [
         pltpu.make_async_copy(src, dst, state_sems.at[i])
         for i, (src, dst) in enumerate(
-            ((step_ref, step_hbm), (first_ref, first_out), (second_ref, second_out))
+            (
+                (step_ref, step_hbm),
+                (first_ref, first_out),
+                (second_ref, second_out),
+                (block_ref, block_out),
+            )
         )
     ]
     for copy in states:
@@ -1279,9 +1301,9 @@
         norm_sum=vmem((3 + bits, 8, width), f32),
         norm_land=vmem((2 + bits, 8, width), f32),
         grads=vmem((3 * width, width), bf16),
-        sum_land=vmem((10, 3 * width // 4, width // 2), bf16),
+        sum_land=vmem((12, 2 * cols + 64, width // 2), bf16),
         send_sems=dma((32,)),
-        recv_sems=dma((20 + 21 * bits,)),
+        recv_sems=dma((20 + 25 * bits,)),
         owner=vmem((1, group), i32),
         rowid=vmem((1, group), i32),
         long=pltpu.SMEM(long_len.shape, i32),
@@ -1330,7 +1352,7 @@
         jax.ShapeDtypeStruct((8, 128), f32),
     )
     if resident:
-        out_shape = out_shape[:1] + (vmem((8, width), f32), vmem((8, 128), f32))
+        out_shape = (vmem((tok, width), bf16), vmem((8, width), f32), vmem((8, 128), f32))
         out_shape += (vmem((3 * width, width), bf16),) + (vmem((table_rows, width), f32),) * 3
         out_specs = (in_vmem,) * 7
     else:
@@ -1380,12 +1402,13 @@
     if resident:
         finished = pl.pallas_call(
             functools.partial(finish_kernel, cols),
-            out_shape=out_shape,
-            in_specs=[in_vmem] * 6,
-            out_specs=out_specs,
-            scratch_shapes=[vmem((3 * width, width), f32), dma((3,)), dma((4,))],
+            out_shape=out_shape + (jax.ShapeDtypeStruct((tok, width), bf16),),
+            in_specs=[in_vmem] * 7,
+            out_specs=out_specs + (in_hbm,),
+            scratch_shapes=[vmem((3 * width, width), f32), dma((4,)), dma((4,))],
             compiler_params=pltpu.CompilerParams(vmem_limit_bytes=20 * 2**20),
-        )(norms, loss, *more)
+        )(block_out, norms, loss, *more)
+        *finished, block_out = finished
     else:
         weights, incoming, ids = more
         parts = 8

time: 208 us -> 196 us (0.942)
  Pallas kernels: 207 us -> 195 us
    pallas_call x1, Pallas kernels: 197 us -> 186 us  [body(): pl.pallas_call(functools.partial(layer_kernel, dims), out_shape=out_shape...]
where the time goes in v3:
time: 196 us
  Pallas kernels  195 us (99%)
    pallas_call x1, Pallas kernels, body(): pl.pallas_call(functools.partial(layer_kernel, dims), out_shape=out_shape...  186 us
    pallas_call x1, Pallas kernels, body(): pl.pallas_call(functools.partial(finish_kernel, cols), out_shape=out_shap...  9.45 us

profile of v3, /device:TPU:0, one launch (start us, length us, event | category | flops | bytes accessed | tf_op | source)
XLA Modules:
  0.0 196.2 jit_solution(1711187111995698605)
XLA Ops:
  0.7 185.9 %shard_map.264 = (bf16[256,768]{1,0:T(8,128)(2,1)S(1)}, f32[8,768]{1,0:T(8,128)S(1)}, f32[8,128]{1,0:T(8,128)S(1)}, bf16[2304,768]{1,0:T(8,128)(2,1)S(1)}, f32[2...) custom-call(s32[1,1024]{1,0:T(1,128)} %bitcast.11, s32[1,1024]{1,0:T(1,128)} %bitcast.12, ...), custom_call_target="tpu_custom_call" | custom-call | tf_op jit(solution)/shard_map/pallas_call | solution.py:1365
  186.6 9.4 %shard_map.265 = (f32[2048,768]{1,0:T(8,128)}, f32[2048,768]{1,0:T(8,128)}, f32[2048,768]{1,0:T(8,128)}, f32[768,768]{1,0:T(8,128)}, f32[768,768]{1,0:T(8,128)},...) custom-call(bf16[256,768]{1,0:T(8,128)(2,1)S(1)} %get-tuple-element., ...), custom_call_target="tpu_custom_call" | custom-call | tf_op jit(solution)/shard_map/pallas_call | solution.py:1403

commit v4 on v3

--- a/solution.py
+++ b/solution.py
@@ -590,7 +590,7 @@
             sums.at[pl.ds(at, rows)],
             s.sum_land.at[i],
             (d, m),
-            bits,
+            bits if i else bits[1::-1] + bits[2:],
         )
         for i, (at, rows) in enumerate(zip(part_at, part_rows, strict=True))
     ]
@@ -653,6 +653,20 @@
 
     scatters = pipeline(gathers, feed)
 
+    gb, gp, gm, gproj = s.gb, s.gp, s.gm, s.gproj
+
+    def second_back(k):
+        rows = own_rows(k)
+        return norm_back(
+            s.grad_rows[rows, :], s.normal_two[rows, :], s.scale_two[rows, 0:1], gain_two
+        )
+
+    def early_gather(k):
+        gb[rows_of(m, k), :] = second_back(k).astype(bf16)
+        gathers.append(Gather(gb, k))
+
+    s.grad_rows[...] = s.upper[...].astype(f32)
+    gathers = []
     for k in range(chunks):
         hidden = s.normed[own_rows(k), :] + scatters[k].end()
         normal, scale = norm_forward(hidden)
@@ -661,20 +675,8 @@
         rows_now = normal * gain_two + shift_two
         s.rows[own_rows(k), :] = rows_now
         block_out[own_rows(k), :] = rows_now.astype(bf16)
-
-    gb, gp, gm, gproj = s.gb, s.gp, s.gm, s.gproj
-
-    def second_back(k):
-        rows = own_rows(k)
-        return norm_back(
-            s.grad_rows[rows, :], s.normal_two[rows, :], s.scale_two[rows, 0:1], gain_two
-        )
-
-    s.grad_rows[...] = s.upper[...].astype(f32)
-    gathers = []
-    for k in range(chunks):
-        gb[rows_of(m, k), :] = second_back(k).astype(bf16)
-        gathers.append(Gather(gb, k))
+        if k < chunks - 1:
+            early_gather(k)
 
     pool = s.pool
     half = width // 2
@@ -683,33 +685,33 @@
     )
     pool[d, m] = jnp.concatenate([firsts[:, :half], firsts[:, half:]], axis=0).astype(bf16)
 
-    def pool_copy(j):
+    def pool_copy(j, model):
         return pltpu.make_async_remote_copy(
             src_ref=pool.at[d, m],
             dst_ref=pool.at[d, m],
             send_sem=s.pool_sems.at[0],
             recv_sem=s.pool_sems.at[1],
-            device_id=(lax.rem(d + j, n_data), m),
+            device_id=(lax.rem(d + j, n_data), model),
             device_id_type=MESH,
         )
 
     def pool_start(j, carry):
-        pool_copy(j).start()
+        pool_copy(j, m).start()
+        pool_copy(j, m2).start()
         return carry
 
     def pool_wait(at):
-        blocks = pool.at[pl.ds(0, n_data - 1), m]
+        blocks = pool.at[pl.ds(0, (2 * n_data - 1) // 3), pl.ds(0, 3)]
         pltpu.make_async_copy(blocks, blocks, s.pool_sems.at[at]).wait()
 
     lax.fori_loop(1, n_data, pool_start, 0)
+    pool_copy(0, m2).start()
+    early_gather(chunks - 1)
     pool_wait(1)
-    far = net.send(pool.at[:, m], pool.at[:, m], by_side)
     near = net.send(pool.at[:, m], pool.at[:, m], by_core)
-    far.wait_recv()
     passed = net.send(pool.at[:, m2], pool.at[:, m2], by_core)
     near.wait_recv()
     passed.wait_recv()
-
 
     count = devices * per_short
     sentences = dims.longs + dims.shorts
@@ -907,9 +909,9 @@
                 first += 1
 
     begin(0, 4, act, gb)
-    scatters = pipeline([], feed_back, middle=((), (0,)))
+    scatters = pipeline([], feed_back, middle=((), (0, 1)))
     begin(4, 8, norm, gp)
-    before_end = ((1, 0), (2, 1, 0))
+    before_end = ((2, 1), (3, 2, 0, 1))
     gathers = []
     for k in range(chunks):
         steps(*before_end[k])
@@ -922,7 +924,7 @@
         gm[rows_of(m, k), :] = back.astype(bf16)
         gathers.append(Gather(gm, k))
     norm_send()
-    steps(3, 2)
+    steps(3, 4, 2, NORM, 0)
 
     def attend_back(k):
         def unmix(at):
@@ -970,14 +972,14 @@
     scatters = pipeline(
         gathers,
         attend_back,
-        forward=((1, NORM, 4, 0), (2, 5, 1, 4)),
-        middle=((NORM, 0, 6), (3, 2, 5, 7, NORM)),
-        finish=((3,), ()),
+        forward=((), (3, 6, 2, 5, NORM, 0, 1, 7, 4, NORM)),
+        middle=((), (2, 5, 1, 7)),
+        finish=((5, 1, 4), (3, 6, 0)),
         also=lambda: begin(8, 9, att, gm, cols),
     )
     begin(9, 12, gproj, x, cols)
-    steps(1, 4, 6, 0)
-    before_end = ((), (3, 2, 8, 5))
+    steps(4, NORM, 8, 3)
+    before_end = ((), (6, NORM, 2))
     swap_sent(s.returned, row_sems)
     for k in range(chunks):
         steps(*before_end[k])
@@ -991,9 +993,9 @@
     tiles(slots, 256, pack)
     swap_start(s.outgoing, s.incoming, out_sems)
 
-    tail = [7, NORM, 9, 4, 6, 3, 10, 8, 5, 11, 1, 2, 9, 7, NORM, 4, 6, 10, 3]
-    rest_of_tail = [8, 5, 11, 4, 9, 7, 6, 5, 10, 8, 11, 9, 7, 6, 10, 8]
-    rest_of_tail += [11, 9, 7, 10, 11, 8, 9, 10, 11]
+    tail = [0, 5, 9, 7, 4, 8, 10, 6, 11, 3, 5, 9, 7]
+    rest_of_tail = [4, 8, 10, 6, 5, 11, 9, 7, 6, 8, 10, 11]
+    rest_of_tail += [9, 8, 7, 10, 11, 9, 10, 8, 11, 9, 10, 11]
     if resident:
         moments = [
             pltpu.make_async_copy(first_hbm, first_out, s.load_sems.at[0]),

time: 196 us -> 191 us (0.974)
  Pallas kernels: 195 us -> 190 us
    pallas_call x1, Pallas kernels: 186 us -> 180 us  [body(): pl.pallas_call(functools.partial(layer_kernel, dims), out_shape=out_shape...]
where the time goes in v4:
time: 191 us; the launch traced here: 190 us
  Pallas kernels  190 us (99%)
    pallas_call x1, Pallas kernels, body(): pl.pallas_call(functools.partial(layer_kernel, dims), out_shape=out_shape...  180 us
    pallas_call x1, Pallas kernels, body(): pl.pallas_call(functools.partial(finish_kernel, cols), out_shape=out_shap...  9.45 us

profile of v4, /device:TPU:0, one launch (start us, length us, event | category | flops | bytes accessed | tf_op | source)
XLA Modules:
  0.0 190.4 jit_solution(2794168940612620990)
XLA Ops:
  0.7 180.1 %shard_map.264 = (bf16[256,768]{1,0:T(8,128)(2,1)S(1)}, f32[8,768]{1,0:T(8,128)S(1)}, f32[8,128]{1,0:T(8,128)S(1)}, bf16[2304,768]{1,0:T(8,128)(2,1)S(1)}, f32[2...) custom-call(s32[1,1024]{1,0:T(1,128)} %bitcast.11, s32[1,1024]{1,0:T(1,128)} %bitcast.12, ...), custom_call_target="tpu_custom_call" | custom-call | tf_op jit(solution)/shard_map/pallas_call | solution.py:1367
  180.7 9.4 %shard_map.265 = (f32[2048,768]{1,0:T(8,128)}, f32[2048,768]{1,0:T(8,128)}, f32[2048,768]{1,0:T(8,128)}, f32[768,768]{1,0:T(8,128)}, f32[768,768]{1,0:T(8,128)},...) custom-call(bf16[256,768]{1,0:T(8,128)(2,1)S(1)} %get-tuple-element., ...), custom_call_target="tpu_custom_call" | custom-call | tf_op jit(solution)/shard_map/pallas_call | solution.py:1405

commit v5 on v4

--- a/solution.py
+++ b/solution.py
@@ -364,12 +364,15 @@
             device_id_type=MESH,
         )
 
-    def swap_start(src, dst, sems):
+    def swap_some(src, dst, sems, first, last):
         def one(j, carry):
             swap_copy(src, dst, sems, other(j)).start()
             return carry
 
-        lax.fori_loop(1, devices, one, 0)
+        lax.fori_loop(first, last, one, 0)
+
+    def swap_start(src, dst, sems):
+        swap_some(src, dst, sems, 1, devices)
         dst[slot_rows(me), :] = src[slot_rows(me), :]
 
     def swap_wait(dst, sem):
@@ -991,7 +994,9 @@
         s.outgoing[rows, :] = nn(s.place[rows, :], s.grad_in[...]).astype(bf16)
 
     tiles(slots, 256, pack)
-    swap_start(s.outgoing, s.incoming, out_sems)
+    batch = devices // 2
+    swap_some(s.outgoing, s.incoming, out_sems, 1, batch)
+    s.incoming[slot_rows(me), :] = s.outgoing[slot_rows(me), :]
 
     tail = [0, 5, 9, 7, 4, 8, 10, 6, 11, 3, 5, 9, 7]
     rest_of_tail = [4, 8, 10, 6, 5, 11, 9, 7, 6, 8, 10, 11]
@@ -1003,6 +1008,10 @@
         ]
         for copy in moments:
             copy.start()
+    for at in range(1, 2):
+        steps(*tail[: 5])
+        tail = tail[5 :]
+        swap_some(s.outgoing, s.incoming, out_sems, at * batch, (at + 1) * batch)
     steps(*tail)
     swap_arrived(s.incoming, out_sems)
     if resident:

time: 191 us -> 190 us (level)
  no operation moved by 1% of the time
where the time goes in v5:
time: 190 us
  Pallas kernels  189 us (99%)
    pallas_call x1, Pallas kernels, body(): pl.pallas_call(functools.partial(layer_kernel, dims), out_shape=out_shape...  180 us
    pallas_call x1, Pallas kernels, body(): pl.pallas_call(functools.partial(finish_kernel, cols), out_shape=out_shap...  9.45 us

profile of v5, /device:TPU:0, one launch (start us, length us, event | category | flops | bytes accessed | tf_op | source)
XLA Modules:
  0.0 190.3 jit_solution(14729276984435424043)
XLA Ops:
  0.7 180.0 %shard_map.264 = (bf16[256,768]{1,0:T(8,128)(2,1)S(1)}, f32[8,768]{1,0:T(8,128)S(1)}, f32[8,128]{1,0:T(8,128)S(1)}, bf16[2304,768]{1,0:T(8,128)(2,1)S(1)}, f32[2...) custom-call(s32[1,1024]{1,0:T(1,128)} %bitcast.11, s32[1,1024]{1,0:T(1,128)} %bitcast.12, ...), custom_call_target="tpu_custom_call" | custom-call | tf_op jit(solution)/shard_map/pallas_call | solution.py:1376
  180.6 9.4 %shard_map.265 = (f32[2048,768]{1,0:T(8,128)}, f32[2048,768]{1,0:T(8,128)}, f32[2048,768]{1,0:T(8,128)}, f32[768,768]{1,0:T(8,128)}, f32[768,768]{1,0:T(8,128)},...) custom-call(bf16[256,768]{1,0:T(8,128)(2,1)S(1)} %get-tuple-element., ...), custom_call_target="tpu_custom_call" | custom-call | tf_op jit(solution)/shard_map/pallas_call | solution.py:1414
